TPU v7x, 512 devices: a whole 4x8x8 slice. The times are simulated.
512 devices in a mesh: tile: 64 (over x, z, core), dp: 8 (over y).
Axes of the slice: x: 4, y: 8, z: 8, core: 2. Of those that a mesh axis runs over, the one named last changes fastest.
Arguments:
- tile_ids: int32 [524288, 1], P(('tile', 'dp')), may hold values from 0 to 63; in each aligned block of 1024 rows (0 to 1023, 1024 to 2047, ...) at most 64 rows name the same one
- corners: int32 [2, 524288], P(None, ('tile', 'dp')), may hold values from 0 to 62
- offsets: float32 [2, 524288], P(None, ('tile', 'dp')), may hold values from 0 to 1
- targets: float32 [3, 32768], P(None, ('tile', 'dp')), may hold values from 0 to 1
- grid: bfloat16 [256, 262144], P('dp', 'tile'), may hold values from -6 to 6
- w_first: bfloat16 [256, 512], replicated, may hold values from -0.375 to 0.375
- w_second: bfloat16 [512, 4], replicated, may hold values from -0.25 to 0.25
Outputs:
- grid_grad: float32 [256, 262144], P('dp', 'tile')
- grad_first: float32 [256, 512], replicated
- grad_second: float32 [512, 4], replicated
Inputs may be any that keep to these rules, and one draw needn't show every extreme that they name: `tile_ids`: among the samples of one device (aligned blocks of 1024 rows) at most 64 name the same tile; in some blocks one tile is named by exactly 64.
All inputs are finite; a program needn't handle non-finite values.
Results may differ from a plain program's by a relative error of at most 0.0041.
The roundings to bfloat16 on the way count: a program that leaves them out, or rounds other values in their place, can miss the bound.
Values may be sent and summed in bfloat16 or wider, within the bound.
No kernel may reach another device: no remote copies, remote signals or barrier semaphores. Data moves between devices by JAX's collectives and lax.ppermute only.
A program may use at most 192 MiB of HBM per device.

v0:
```python
import jax
import jax.numpy as jnp
from jax import lax
from jax.sharding import PartitionSpec as P

GSIDE = 64
MARCH = 15


march_step = 0.1
ambient = 0.3


def corner_weights(offsets):
    along = offsets[0]
    across = offsets[1]
    stacked = jnp.stack(
        [
            (1.0 - along) * (1.0 - across),
            (1.0 - along) * across,
            along * (1.0 - across),
            along * across,
        ]
    )
    return stacked.astype(jnp.bfloat16)


def shade_grads(features, w_first, w_second, wanted):
    pre_act = jnp.dot(features, w_first, preferred_element_type=jnp.float32)
    hidden = jax.nn.silu(pre_act).astype(jnp.bfloat16)
    decoded = jnp.dot(hidden, w_second, preferred_element_type=jnp.float32)
    ray_count = wanted.shape[1]
    decoded = decoded.reshape(ray_count, MARCH + 1, 4)
    raw_density = decoded[:, 1:, 0]
    density = jax.nn.softplus(raw_density)
    transmit = jnp.exp(-march_step * jnp.sum(density, axis=1))
    albedo = jax.nn.sigmoid(decoded[:, 0, 1:])
    lighting = ambient + (1.0 - ambient) * transmit
    errors = albedo * lighting[:, None] - wanted.T
    albedo_grad = errors * lighting[:, None]
    transmit_grad = (1.0 - ambient) * jnp.sum(errors * albedo, axis=1)
    march_grad = (-march_step * transmit * transmit_grad)[:, None] * jax.nn.sigmoid(raw_density)
    surface_grad = jnp.concatenate(
        [jnp.zeros((ray_count, 1), jnp.float32), albedo_grad * albedo * (1.0 - albedo)], axis=1
    )
    sun_grad = jnp.concatenate(
        [march_grad[:, :, None], jnp.zeros((ray_count, MARCH, 3), jnp.float32)], axis=2
    )
    decoded_grad = jnp.concatenate([surface_grad[:, None, :], sun_grad], axis=1).reshape(-1, 4)
    grad_second = jnp.dot(
        hidden.astype(jnp.float32).T, decoded_grad, precision=lax.Precision.HIGHEST
    )
    hidden_grad = jnp.dot(
        decoded_grad, w_second.astype(jnp.float32).T, precision=lax.Precision.HIGHEST
    )
    smooth_gate = jax.nn.sigmoid(pre_act)
    pre_grad = (hidden_grad * smooth_gate * (1.0 + pre_act * (1.0 - smooth_gate))).astype(
        jnp.bfloat16
    )
    grad_first = lax.dot_general(
        features, pre_grad, (((0,), (0,)), ((), ())), preferred_element_type=jnp.float32
    )
    feature_grad = lax.dot_general(
        pre_grad, w_first, (((1,), (1,)), ((), ())), preferred_element_type=jnp.float32
    )
    return (grad_first, grad_second, feature_grad.astype(jnp.bfloat16))


def corner_list(base_cell):
    corner_shift = jnp.array([0, 1, GSIDE, GSIDE + 1], dtype=jnp.int32)
    return base_cell[None, :] + corner_shift[:, None]


def interpolate(base_cell, weights, grid_table):
    cell_rows = grid_table.T
    corner_cells = corner_list(base_cell)
    total = jnp.zeros((base_cell.shape[0], grid_table.shape[0]), jnp.float32)
    for corner in range(4):
        picked = cell_rows[corner_cells[corner]].astype(jnp.float32)
        total = total + picked * weights[corner].astype(jnp.float32)[:, None]
    return total


def spread(base_cell, weights, grads, cell_count):
    channels = grads.shape[1]
    corner_cells = corner_list(base_cell)
    grads_wide = grads.astype(jnp.float32)
    total = jnp.zeros((cell_count, channels), jnp.float32)
    for corner in range(4):
        total = total.at[corner_cells[corner]].add(
            weights[corner].astype(jnp.float32)[:, None] * grads_wide
        )
    return total.T


def body(tile_ids, corners, offsets, targets, grid, w_first, w_second):
    owners = lax.axis_size("tile")
    samples = tile_ids.shape[0]
    capacity = 4 * samples // owners
    slot_count = owners * capacity
    cell_count = grid.shape[1]
    tile_index = tile_ids[:, 0]
    members = (tile_index[:, None] == jnp.arange(owners, dtype=jnp.int32)[None, :]).astype(
        jnp.int32
    )
    earlier = jnp.cumsum(members, axis=0) - members
    ranking = jnp.sum(earlier * members, axis=1)
    slot_of = tile_index * capacity + ranking
    base_cell = corners[0] * GSIDE + corners[1]
    weights = corner_weights(offsets)
    send_cells = jnp.zeros((1, slot_count), jnp.int32).at[0, slot_of].set(base_cell)
    send_weights = jnp.zeros((4, slot_count), jnp.bfloat16).at[:, slot_of].set(weights)
    recv_cells, recv_weights = (
        lax.all_to_all(send_cells, "tile", split_axis=1, concat_axis=1, tiled=True),
        lax.all_to_all(send_weights, "tile", split_axis=1, concat_axis=1, tiled=True),
    )
    grid_table = lax.all_gather(grid, "dp", axis=0, tiled=True)
    values = interpolate(recv_cells[0], recv_weights, grid_table).astype(jnp.bfloat16)
    returned = lax.all_to_all(values, "tile", split_axis=0, concat_axis=0, tiled=True)
    features = returned[slot_of]
    grad_first, grad_second, feature_grad = shade_grads(features, w_first, w_second, targets)
    grad_slots = (
        jnp.zeros((slot_count, feature_grad.shape[1]), jnp.bfloat16).at[slot_of].set(feature_grad)
    )
    owner_grads = lax.all_to_all(grad_slots, "tile", split_axis=0, concat_axis=0, tiled=True)
    full_grad = spread(recv_cells[0], recv_weights, owner_grads, cell_count)
    grid_grad = lax.psum_scatter(full_grad, "dp", scatter_dimension=0, tiled=True)
    grad_first, grad_second = lax.psum((grad_first, grad_second), ("tile", "dp"))
    return (grid_grad, grad_first, grad_second)


def solution(mesh):
    in_specs = (
        P(("tile", "dp"), None),
        P(None, ("tile", "dp")),
        P(None, ("tile", "dp")),
        P(None, ("tile", "dp")),
        P("dp", "tile"),
        P(),
        P(),
    )
    out_specs = (P("dp", "tile"), P(), P())
    return jax.shard_map(body, mesh=mesh, in_specs=in_specs, out_specs=out_specs, check_vma=False)
```

profile of v0, /device:TPU:1, one launch (start us, length us, event | category | flops | bytes accessed | tf_op | source)
XLA Modules:
  0.0 584.2 jit_solution(113058298329536216)
XLA Ops:
  7.2 0.7 all-gather.2.cloned.1.call-update
  7.9 0.8 slice_add_fusion
  8.7 0.7 fusion.20
  9.4 18.0 %reduce-window.6 = s32[64,8,128]{2,1,0:T(8,128)S(1)} reduce-window(s32[64,8,128]{2,1,0:T(8,128)S(1)} %fusion.20, s32[]{:T(128)} %constant.11.clone.1), window={size=1x1x128 pad=0_0x0_0x127_0}, to_apply=%region_0.0 | reduce-window | flops 8323072 | bytes 524292 | tf_op jit(solution)/shard_map/reduce-window
  27.4 0.1 slice.98
  27.6 0.1 copy.61
  27.8 0.1 copy.62
  27.8 0.1 broadcast_add_fusion
  28.0 0.8 fusion.19
  28.7 0.7 compare_select_fusion.5
  29.5 0.8 and_reduce_fusion
  30.2 0.7 fusion.26
  31.0 4.3 scatter_custom_fusion.6
  35.3 0.7 all_to_all.24
  36.0 14.8 %all-to-all-start = ((s32[1,64,64]{2,0,1:T(1,128)}), s32[1,64,64]{2,0,1:T(1,128)S(1)}, u32[]{:S(2)}, u32[]{:S(2)}) async-start(s32[1,64,64]{2,0,1:T(1,128)} %all_to_all.24), calls=%async_computation | async-start | bytes 65536 | tf_op jit(solution)/shard_map/all_to_all | solution.py:114
  50.8 0.8 multiply_convert_fusion.5
  51.7 0.2 copy.63
  51.9 3.5 scatter_custom_fusion
  55.4 0.5 copy.64
  55.9 0.7 reshape.514
  56.6 3.4 all-to-all-done
  60.1 6.9 %all-to-all-start.1 = ((bf16[64,2,128]{2,1,0:T(2,128)(2,1)}), bf16[64,2,128]{2,1,0:T(2,128)(2,1)S(1)}, u32[]{:S(2)}, u32[]{:S(2)}) async-start(bf16[64,2,128]{2,1,0:T(2,128)(2,1)} %reshape.514), calls=%async_computation.1 | async-start | bytes 65536 | tf_op jit(solution)/shard_map/all_to_all | solution.py:115
  66.9 0.5 broadcast.307
  67.5 0.7 reduce.7
  68.3 0.1 broadcast_add_fusion.1
  68.4 0.1 compare_select_fusion.2
  68.5 7.6 %all-to-all-done.1 = bf16[64,2,128]{2,1,0:T(2,128)(2,1)S(1)} async-done(((bf16[64,2,128]{2,1,0:T(2,128)(2,1)}), bf16[64,2,128]{2,1,0:T(2,128)(2,1)S(1)}, u32[]{:S(2)}, u32[]{:S(2)}) %all-to-all-start.1) | async-done | bytes 32800 | tf_op jit(solution)/shard_map/all_to_all | solution.py:115
  76.2 0.1 reshape.515
  76.3 0.1 fusion.36
  76.5 3.3 copy.66
  79.8 16.9 %gather_fusion = bf16[4096,256]{1,0:T(8,128)(2,1)} fusion(bf16[4096,256]{1,0:T(8,128)(2,1)S(1)} %bitcast.132, s32[4096]{0:T(1024)S(1)} %broadcast_clamp_fusion.3), kind=kCustom, calls=%fused_computation | custom fusion | bytes 4210688 | tf_op jit(solution)/shard_map/gather | solution.py:79
  96.7 16.9 %gather_fusion.2 = bf16[4096,256]{1,0:T(8,128)(2,1)} fusion(bf16[4096,256]{1,0:T(8,128)(2,1)S(1)} %bitcast.133, s32[4096]{0:T(1024)S(1)} %broadcast_clamp_fusion.1), kind=kCustom, calls=%fused_computation.2 | custom fusion | bytes 4210688 | tf_op jit(solution)/shard_map/gather | solution.py:79
  113.6 16.9 %gather_fusion.1 = bf16[4096,256]{1,0:T(8,128)(2,1)} fusion(bf16[4096,256]{1,0:T(8,128)(2,1)S(1)} %bitcast.134, s32[4096]{0:T(1024)S(1)} %broadcast_clamp_fusion.2), kind=kCustom, calls=%fused_computation.1 | custom fusion | bytes 4210688 | tf_op jit(solution)/shard_map/gather | solution.py:79
  130.5 16.9 %gather_fusion.3 = bf16[4096,256]{1,0:T(8,128)(2,1)} fusion(bf16[4096,256]{1,0:T(8,128)(2,1)S(1)} %bitcast.135, s32[4096]{0:T(1024)S(1)} %broadcast_clamp_fusion), kind=kCustom, calls=%fused_computation.3 | custom fusion | bytes 4210688 | tf_op jit(solution)/shard_map/gather | solution.py:79
  147.4 7.0 %fusion.5 = bf16[64,64,256]{2,1,0:T(8,128)(2,1)} fusion(bf16[64,64,256]{2,1,0:T(8,128)(2,1)} %bitcast.146, bf16[64,64,256]{2,1,0:T(8,128)(2,1)} %bitcast.144, bf16[64,64,256]{2,1,0:T(8,128)(2,1)} %bitcast.145, bf16[64,64,256]{2,1,0:T(8,128)(2,1)} %bitcast.143, f32[64,64]{1,0:T(8,128)S(1)} %get-tuple-element.30, f32[64,64]{1,0:T(8,128)S(1)} %get-tuple-element.45, ...), kind=kLoop, calls=%fused_computation.22 | loop fusion | flops 12582912 | bytes 10551296 | tf_op jit(solution)/shard_map/convert_element_type | solution.py:118
  154.5 4.8 all-to-all-start.2
  159.3 51.3 %all-to-all-done.2 = bf16[64,64,256]{2,1,0:T(8,128)(2,1)S(1)} async-done(((bf16[64,64,256]{2,1,0:T(8,128)(2,1)}), bf16[64,64,256]{2,1,0:T(8,128)(2,1)S(1)}, u32[]{:S(2)}, u32[]{:S(2)}) %all-to-all-start.2) | async-done | bytes 2097184 | tf_op jit(solution)/shard_map/all_to_all | solution.py:119
  210.6 3.9 gather_fusion.4
  214.6 2.0 multiply_convert_fusion.1
  216.6 1.1 copy-done.1
  217.7 0.4 fusion.37
  218.1 0.1 reshape.375
  218.2 0.2 fusion.21
  218.4 0.1 copy.82
  218.6 0.1 divide_multiply_fusion
  218.7 0.1 copy.71
  218.8 0.1 select_maximum_fusion
  218.9 0.1 reshape.376
  219.0 3.1 multiply_convert_fusion
  222.2 0.5 convolution_convert_fusion
  222.6 6.8 %scatter_custom_fusion.1 = bf16[4096,256]{1,0:T(8,128)(2,1)} fusion(s32[1024]{0:T(1024)} %bitcast.153, bf16[1024,256]{1,0:T(8,128)(2,1)S(1)} %convolution_convert_fusion, bf16[]{:T(256)} %constant.14.clone.1), kind=kCustom, calls=%fused_computation.37 | custom fusion | bytes 2097664 | tf_op jit(solution)/shard_map/scatter | solution.py:123
  229.4 5.8 all-to-all-start.3
  235.3 2.3 fusion.38
  237.9 49.0 %all-to-all-done.3 = bf16[64,64,256]{2,1,0:T(8,128)(2,1)S(1)} async-done(((bf16[64,64,256]{2,1,0:T(8,128)(2,1)}), bf16[64,64,256]{2,1,0:T(8,128)(2,1)S(1)}, u32[]{:S(2)}, u32[]{:S(2)}) %all-to-all-start.3) | async-done | bytes 2097184 | tf_op jit(solution)/shard_map/all_to_all | solution.py:125
  286.9 30.9 %scatter_custom_fusion.2 = f32[4096,256]{1,0:T(8,128)} fusion(s32[4096]{0:T(1024)} %bitcast.161, bf16[4096,256]{1,0:T(8,128)(2,1)S(1)} %bitcast.136, f32[4096]{0:T(1024)S(1)} %reshape.382, f32[]{:T(128)} %constant.10.clone.1), kind=kCustom, calls=%fused_computation.16 | custom fusion | flops 3145728 | bytes 6308352 | tf_op jit(solution)/shard_map/scatter-add | solution.py:90
  317.8 32.9 %scatter_custom_fusion.3 = f32[4096,256]{1,0:T(8,128)} fusion(f32[4096,256]{1,0:T(8,128)} %scatter_custom_fusion.2, s32[4096]{0:T(1024)} %bitcast.159, bf16[4096,256]{1,0:T(8,128)(2,1)S(1)} %bitcast.137, f32[4096]{0:T(1024)S(1)} %reshape.392), kind=kCustom, calls=%fused_computation.17 | custom fusion | flops 3145728 | bytes 6307840 | tf_op jit(solution)/shard_map/scatter-add | solution.py:90
  350.7 32.9 %scatter_custom_fusion.4 = f32[4096,256]{1,0:T(8,128)} fusion(f32[4096,256]{1,0:T(8,128)} %scatter_custom_fusion.3, s32[4096]{0:T(1024)} %bitcast.157, bf16[4096,256]{1,0:T(8,128)(2,1)S(1)} %bitcast.138, f32[4096]{0:T(1024)S(1)} %reshape.393), kind=kCustom, calls=%fused_computation.18 | custom fusion | flops 3145728 | bytes 6307840 | tf_op jit(solution)/shard_map/scatter-add | solution.py:90
  383.5 32.9 %scatter_custom_fusion.5 = f32[4096,256]{1,0:T(8,128)} fusion(f32[4096,256]{1,0:T(8,128)} %scatter_custom_fusion.4, s32[4096]{0:T(1024)} %bitcast.155, bf16[4096,256]{1,0:T(8,128)(2,1)S(1)} %bitcast.139, f32[4096]{0:T(1024)S(1)} %reshape.394), kind=kCustom, calls=%fused_computation.19 | custom fusion | flops 3145728 | bytes 6307840 | tf_op jit(solution)/shard_map/scatter-add | solution.py:90
  416.4 5.6 copy.73
  422.1 1.2 copy-done.2
  423.3 0.5 fusion.39
  423.8 99.0 %psum.15 = f32[512,4]{0,1:T(4,128)} all-reduce(f32[512,4]{0,1:T(4,128)S(1)} %fusion.39), channel_id=1, replica_groups=mesh['tile'=64,'dp'=8] {'tile','dp'}, use_global_device_ids=true, to_apply=%region_14.15 | all-reduce | flops 2048 | bytes 16384 | tf_op jit(solution)/shard_map/psum | solution.py:128
  522.8 53.0 %reduce-scatter.4.cloned.1.call-done = f32[32,4096]{1,0:T(8,128)} async-done(((f32[256,4096]{1,0:T(8,128)}), f32[32,4096]{1,0:T(8,128)}) %reduce-scatter.4.cloned.1.call-update) | async-done | bytes 524304
  575.8 1.9 copy.116
  (50 shorter events, 0.8 us)
Async XLA Ops:
  7.2 207.4 %copy-start = (bf16[256,512]{1,0:T(8,128)(2,1)S(1)}, bf16[256,512]{1,0:T(8,128)(2,1)}, u32[]{:S(2)}) copy-start(bf16[256,512]{1,0:T(8,128)(2,1)} %param.14) | copy-start | bytes 786436
  7.2 61.1 %copy-start.11 = (s32[4]{0:T(128)S(1)}, s32[4]{0:T(128)}, u32[]{:S(2)}) copy-start(s32[4]{0:T(128)} %constant.19.clone) | copy-start | bytes 52
  7.2 69.3 %all-gather.2.cloned.1.call-start = ((), (), s32[]{:S(2)}) async-start(), calls=%async_computation.5 | async-start | bytes 2359296 | tf_op jit(solution)/shard_map/all_gather | solution.py:117
  29.4 129.8 %copy-start.4 = (s32[1024,1]{0,1:T(1,128)}, s32[1024,1]{0,1:T(1,128)S(1)}, u32[]{:S(2)}) copy-start(s32[1024,1]{0,1:T(1,128)S(1)} %compare_select_fusion.5) | copy-start | bytes 12292
  36.0 24.1 %all-to-all-start = ((s32[1,64,64]{2,0,1:T(1,128)}), s32[1,64,64]{2,0,1:T(1,128)S(1)}, u32[]{:S(2)}, u32[]{:S(2)}) async-start(s32[1,64,64]{2,0,1:T(1,128)} %all_to_all.24), calls=%async_computation | async-start | bytes 65536 | tf_op jit(solution)/shard_map/all_to_all | solution.py:114
  60.1 16.1 %all-to-all-start.1 = ((bf16[64,2,128]{2,1,0:T(2,128)(2,1)}), bf16[64,2,128]{2,1,0:T(2,128)(2,1)S(1)}, u32[]{:S(2)}, u32[]{:S(2)}) async-start(bf16[64,2,128]{2,1,0:T(2,128)(2,1)} %reshape.514), calls=%async_computation.1 | async-start | bytes 65536 | tf_op jit(solution)/shard_map/all_to_all | solution.py:115
  68.4 7.8 %copy-start.5 = (s32[4096,1]{0,1:T(1,128)}, s32[4096,1]{0,1:T(1,128)S(1)}, u32[]{:S(2)}) copy-start(s32[4096,1]{0,1:T(1,128)S(1)} %get-tuple-element.26) | copy-start | bytes 49156
  68.5 7.8 %copy-start.6 = (s32[4096,1]{0,1:T(1,128)}, s32[4096,1]{0,1:T(1,128)S(1)}, u32[]{:S(2)}) copy-start(s32[4096,1]{0,1:T(1,128)S(1)} %get-tuple-element.27) | copy-start | bytes 49156
  68.5 7.8 %copy-start.7 = (s32[4096,1]{0,1:T(1,128)}, s32[4096,1]{0,1:T(1,128)S(1)}, u32[]{:S(2)}) copy-start(s32[4096,1]{0,1:T(1,128)S(1)} %get-tuple-element.25) | copy-start | bytes 49156
  68.5 7.8 %copy-start.8 = (s32[4096,1]{0,1:T(1,128)}, s32[4096,1]{0,1:T(1,128)S(1)}, u32[]{:S(2)}) copy-start(s32[4096,1]{0,1:T(1,128)S(1)} %get-tuple-element.28) | copy-start | bytes 49156
  154.5 56.2 %all-to-all-start.2 = ((bf16[64,64,256]{2,1,0:T(8,128)(2,1)}), bf16[64,64,256]{2,1,0:T(8,128)(2,1)S(1)}, u32[]{:S(2)}, u32[]{:S(2)}) async-start(bf16[64,64,256]{2,1,0:T(8,128)(2,1)} %fusion.5), calls=%async_computation.2 | async-start | bytes 4194304 | tf_op jit(solution)/shard_map/all_to_all | solution.py:119
  214.6 2.0 copy-start.3
  214.6 3.1 copy-start.9
  214.6 3.9 copy-start.10
  216.6 1.1 copy-start.1
  229.4 57.5 %all-to-all-start.3 = ((bf16[64,64,256]{2,1,0:T(8,128)(2,1)}), bf16[64,64,256]{2,1,0:T(8,128)(2,1)S(1)}, u32[]{:S(2)}, u32[]{:S(2)}) async-start(bf16[64,64,256]{2,1,0:T(8,128)(2,1)} %bitcast.142), calls=%async_computation.3 | async-start | bytes 4194304 | tf_op jit(solution)/shard_map/all_to_all | solution.py:125
  235.2 287.6 %all-reduce.5.cloned.1.call-start = ((), (), s32[]{:S(2)}) async-start(), calls=%async_computation.6 | async-start | bytes 1048576 | tf_op jit(solution)/shard_map/psum | solution.py:128
  237.6 338.2 %reduce-scatter.4.cloned.1.call-start = ((), (), s32[]{:S(2)}) async-start(), calls=%async_computation.7 | async-start | bytes 4718592
  422.1 1.2 copy-start.2
Sparse Core Ops, SparseCore 0:
  10.1 45.5 all-gather.1
  241.6 276.5 all-reduce.4
  521.8 53.8 reduce-scatter.3
where the time goes:
time: 585 us; the launch traced here: 584 us
  waiting for transfers between devices  165 us (28%)
  other arithmetic  161 us (28%)
  local copies, waits for them, and re-layouts  103 us (18%)
  blocking collectives  99 us (17%)
  starting transfers between devices  32.5 us (6%)
  between operations  14.2 us (2%)
  matrix products  8.76 us (1%)
    scatter-add x4, other arithmetic, spread(): total.at[corner_cells[corner]]  130 us
    psum x1, blocking collectives, body(): lax.psum((grad_first, grad_second), ('tile', 'dp'))  99 us
    gather x4, local copies, waits for them, and re-layouts, interpolate(): picked = cell_rows[corner_cells[corner]].astype(jnp.float32)  67.7 us
    unnamed x4, waiting for transfers between devices  53.7 us
    all_to_all x1, waiting for transfers between devices, body(): lax.all_to_all(values, 'tile', split_axis=0, concat_axis=0, tiled=True)  51.3 us
    all_to_all x1, waiting for transfers between devices, body(): lax.all_to_all(grad_slots, 'tile', split_axis=0, concat_axis=0, tiled=True)  49 us
    another operation x4, other arithmetic  19 us
    unnamed x30, local copies, waits for them, and re-layouts  15.1 us
  transfers between devices with their start and end apart: 7, of which 5 were waited for; matrix products, arithmetic and copies ran while one was open for 30% of the time, Pallas kernels for 0%

commit v1 on v0

v1 whole, which is shorter than its diff:
```python
import functools

import jax
import jax.numpy as jnp
from jax import lax
from jax.experimental import pallas as pl
from jax.experimental.pallas import tpu as pltpu
from jax.sharding import PartitionSpec as P

GSIDE = 64
MARCH = 15
march_step = 0.1
ambient = 0.3

bf16 = jnp.bfloat16
f32 = jnp.float32
HIGHEST = lax.Precision.HIGHEST
FIELDS = 6
VMEM_BYTES = 56 << 20


def matmul(a, b, dims=((1,), (0,)), precision=None):
    return lax.dot_general(a, b, (dims, ((), ())), precision=precision, preferred_element_type=f32)


def row_iota(shape, dim):
    return lax.broadcasted_iota(jnp.int32, shape, dim)


def slot_kernel(tile_ref, corners_ref, offsets_ref, send_ref, rank_ref, *, tiles, capacity):
    tile = tile_ref[...]
    samples = tile.shape[1]
    members = row_iota((tiles, samples), 0) == tile
    member_rows = members.astype(f32).astype(bf16)
    before = (
        row_iota((samples, samples), 0) < row_iota((samples, samples), 1)
    ).astype(f32).astype(bf16)
    earlier = matmul(member_rows, before)
    rank = jnp.sum(jnp.where(members, earlier, 0.0), axis=0, keepdims=True)
    rank_ref[...] = rank
    at_rank = row_iota((capacity, samples), 0) == rank.astype(jnp.int32)
    along = offsets_ref[0:1]
    across = offsets_ref[1:2]
    fields = [
        corners_ref[0:1].astype(f32),
        corners_ref[1:2].astype(f32),
        (1.0 - along) * (1.0 - across),
        (1.0 - along) * across,
        along * (1.0 - across),
        along * across,
    ]
    for number, field in enumerate(fields):
        placed = jnp.where(at_rank, field, 0.0).astype(bf16)
        send_ref[number] = matmul(member_rows, placed, ((1,), (1,))).astype(bf16)


def sample_columns(info):
    slots = info.shape[1]
    col = row_iota((GSIDE, slots), 0).astype(f32).astype(bf16)

    def full(number):
        return jnp.broadcast_to(info[number : number + 1], (GSIDE, slots))

    zero = jnp.zeros((GSIDE, slots), bf16)
    here = col == full(1)
    after = col == full(1) + jnp.ones((), bf16)
    upper = jnp.where(here, full(2), jnp.where(after, full(3), zero))
    lower = jnp.where(here, full(4), jnp.where(after, full(5), zero))
    return full(0), upper, lower


def weight_rows(row, upper, lower, count):
    zero = jnp.zeros_like(upper)
    for a in range(count):
        yield a, jnp.where(row == float(a), upper, jnp.where(row == float(a - 1), lower, zero))


def forward_kernel(
    info_ref, grid_ref, first_t_ref, second_t_ref,
    features_ref, hidden_ref, slope_ref, decoded_ref, weights_ref,
):
    row, upper, lower = sample_columns(info_ref[...])
    for a, piece in weight_rows(row, upper, lower, GSIDE):
        weights_ref[pl.ds(a * GSIDE, GSIDE), :] = piece
    features = matmul(grid_ref[...], weights_ref[...]).astype(bf16)
    features_ref[...] = features
    pre_act = matmul(first_t_ref[...], features)
    gate = jax.nn.sigmoid(pre_act)
    hidden = (pre_act * gate).astype(bf16)
    hidden_ref[...] = hidden
    slope_ref[...] = gate * (1.0 + pre_act * (1.0 - gate))
    decoded_ref[...] = matmul(second_t_ref[...], hidden)[0:8]


def forward_call(info, grid_table, first_t, second_t, block=1024):
    channels, cells = grid_table.shape
    hid = first_t.shape[0]
    slots = info.shape[1]
    whole = lambda s: (0, 0)
    part = lambda s: (0, s)
    return pl.pallas_call(
        forward_kernel,
        grid=(slots // block,),
        in_specs=[
            pl.BlockSpec((16, block), part),
            pl.BlockSpec((channels, cells), whole),
            pl.BlockSpec((hid, channels), whole),
            pl.BlockSpec((16, hid), whole),
        ],
        out_specs=[
            pl.BlockSpec((channels, block), part),
            pl.BlockSpec((hid, block), part),
            pl.BlockSpec((hid, block), part),
            pl.BlockSpec((8, block), part),
        ],
        out_shape=[
            jax.ShapeDtypeStruct((channels, slots), bf16),
            jax.ShapeDtypeStruct((hid, slots), bf16),
            jax.ShapeDtypeStruct((hid, slots), f32),
            jax.ShapeDtypeStruct((8, slots), f32),
        ],
        scratch_shapes=[pltpu.VMEM((cells, block), bf16)],
        compiler_params=pltpu.CompilerParams(vmem_limit_bytes=VMEM_BYTES),
    )(info, grid_table, first_t, second_t)


def shade_kernel(tile_ref, rank_ref, back_ref, targets_ref, send_ref, *, tiles, capacity):
    tile = tile_ref[...]
    samples = tile.shape[1]
    rays = targets_ref.shape[1]
    members = (row_iota((tiles, samples), 0) == tile).astype(f32)
    at_rank = row_iota((capacity, samples), 0) == rank_ref[...].astype(jnp.int32)
    decoded = []
    for number in range(4):
        spread = matmul(back_ref[number], members, ((0,), (0,)), HIGHEST)
        decoded.append(jnp.sum(jnp.where(at_rank, spread, 0.0), axis=0, keepdims=True))
    raw = decoded[0]
    ray_of = row_iota((rays, samples), 1) // (MARCH + 1) == row_iota((rays, samples), 0)
    first = row_iota((rays, samples), 1) == row_iota((rays, samples), 0) * (MARCH + 1)
    on_march = jnp.where(ray_of & ~first, 1.0, 0.0)
    on_surface = jnp.where(first, 1.0, 0.0)
    density = jnp.maximum(raw, 0.0) + jnp.log1p(jnp.exp(-jnp.abs(raw)))
    along_rays = ((1,), (1,))
    total = matmul(jnp.broadcast_to(density, (8, samples)), on_march, along_rays, HIGHEST)[0:1]
    colours = jnp.concatenate(decoded[1:] + [jnp.zeros((5, samples), f32)], axis=0)
    surface = matmul(colours, on_surface, along_rays, HIGHEST)
    transmit = jnp.exp(-march_step * total)
    lighting = ambient + (1.0 - ambient) * transmit
    albedo = jax.nn.sigmoid(surface[0:3])
    errors = albedo * lighting - targets_ref[...]
    surface_grad = errors * lighting * albedo * (1.0 - albedo)
    transmit_grad = (1.0 - ambient) * jnp.sum(errors * albedo, axis=0, keepdims=True)
    march_grad = -march_step * transmit * transmit_grad
    march_all = matmul(jnp.broadcast_to(march_grad, (8, rays)), on_march, precision=HIGHEST)[0:1]
    surface_all = matmul(
        jnp.concatenate([surface_grad, jnp.zeros((5, rays), f32)], axis=0),
        on_surface,
        precision=HIGHEST,
    )
    grads = [march_all * jax.nn.sigmoid(raw)] + [surface_all[k : k + 1] for k in range(3)]
    for number in range(4):
        placed = jnp.where(at_rank, grads[number], 0.0)
        send_ref[number] = matmul(members, placed, along_rays, HIGHEST)


def backward_kernel(
    grads_ref, hidden_ref, slope_ref, features_ref, first_ref, second_ref,
    feature_grad_ref, grad_first_ref, grad_second_ref,
):
    @pl.when(pl.program_id(0) == 0)
    def _():
        grad_first_ref[...] = jnp.zeros_like(grad_first_ref)
        grad_second_ref[...] = jnp.zeros_like(grad_second_ref)

    grads = grads_ref[...]
    high = grads.astype(bf16).astype(f32)
    rest = grads - high
    mid = rest.astype(bf16).astype(f32)
    low = rest - mid
    pieces = jnp.concatenate([high, mid, low], axis=0).astype(bf16)
    pre_grad = (matmul(second_ref[...], pieces) * slope_ref[...]).astype(bf16)
    feature_grad_ref[...] = matmul(first_ref[...], pre_grad).astype(bf16)
    grad_first_ref[...] += matmul(features_ref[...], pre_grad, ((1,), (1,)))
    three = matmul(pieces, hidden_ref[...], ((1,), (1,)))
    grad_second_ref[...] += three[0:8] + three[8:16] + three[16:24]


def backward_call(grads, hidden, slope, features, first, second, block=1024):
    hid, slots = hidden.shape
    channels = features.shape[0]
    whole = lambda s: (0, 0)
    part = lambda s: (0, s)
    return pl.pallas_call(
        backward_kernel,
        grid=(slots // block,),
        in_specs=[
            pl.BlockSpec((8, block), part),
            pl.BlockSpec((hid, block), part),
            pl.BlockSpec((hid, block), part),
            pl.BlockSpec((channels, block), part),
            pl.BlockSpec((channels, hid), whole),
            pl.BlockSpec((hid, 24), whole),
        ],
        out_specs=[
            pl.BlockSpec((channels, block), part),
            pl.BlockSpec((channels, hid), whole),
            pl.BlockSpec((8, hid), whole),
        ],
        out_shape=[
            jax.ShapeDtypeStruct((channels, slots), bf16),
            jax.ShapeDtypeStruct((channels, hid), f32),
            jax.ShapeDtypeStruct((8, hid), f32),
        ],
        compiler_params=pltpu.CompilerParams(vmem_limit_bytes=VMEM_BYTES),
    )(grads, hidden, slope, features, first, second)


def spread_kernel(info_ref, grads_ref, out_ref, weights_ref, *, cell_block, slot_block):
    rows = cell_block // GSIDE
    start = jnp.full((1, 1), pl.program_id(0) * rows, jnp.int32).astype(f32).astype(bf16)
    for s in range(0, info_ref.shape[1], slot_block):
        row, upper, lower = sample_columns(info_ref[:, s : s + slot_block])
        for a, piece in weight_rows(row - start, upper, lower, rows):
            weights_ref[pl.ds(a * GSIDE, GSIDE), s : s + slot_block] = piece
    out_ref[...] = matmul(grads_ref[...], weights_ref[...], ((1,), (1,)))


def spread_call(info, grads, cells, cell_block=1024, slot_block=512):
    channels, slots = grads.shape
    whole = lambda s: (0, 0)
    return pl.pallas_call(
        functools.partial(spread_kernel, cell_block=cell_block, slot_block=slot_block),
        grid=(cells // cell_block,),
        in_specs=[pl.BlockSpec((16, slots), whole), pl.BlockSpec((channels, slots), whole)],
        out_specs=pl.BlockSpec((channels, cell_block), lambda s: (0, s)),
        out_shape=jax.ShapeDtypeStruct((channels, cells), f32),
        scratch_shapes=[pltpu.VMEM((cell_block, slots), bf16)],
        compiler_params=pltpu.CompilerParams(vmem_limit_bytes=VMEM_BYTES),
    )(info, grads)


def over_tile(x):
    return lax.all_to_all(x, "tile", split_axis=0, concat_axis=0, tiled=True)


def to_peers(x):
    fields, peers, capacity = x.shape
    return over_tile(x.transpose(1, 0, 2).reshape(peers, fields * capacity))


def from_peers(x, fields):
    peers = x.shape[0]
    return x.reshape(peers, fields, x.shape[1] // fields).transpose(1, 0, 2)


def all_sum(grad_first, grad_second):
    owners = lax.axis_size("tile")
    groups = lax.axis_size("dp")
    flat_first = grad_first.reshape(owners, -1)
    width = flat_first.shape[1]
    flat = jnp.concatenate([flat_first, grad_second.reshape(owners, -1)], axis=1)
    mine = jnp.sum(over_tile(flat), axis=0, keepdims=True)
    copies = jnp.broadcast_to(mine, (groups, mine.shape[1]))
    shared = lax.all_to_all(copies, "dp", split_axis=0, concat_axis=0, tiled=True)
    summed = jnp.sum(shared, axis=0, keepdims=True)
    everything = over_tile(jnp.broadcast_to(summed, (owners, summed.shape[1])))
    first = everything[:, :width].reshape(grad_first.shape)
    second = everything[:, width:].reshape(grad_second.shape)
    return first, second.T


def body(tile_ids, corners, offsets, targets, grid, w_first, w_second):
    owners = lax.axis_size("tile")
    samples = tile_ids.shape[0]
    capacity = 4 * samples // owners
    slot_count = owners * capacity
    cells = grid.shape[1]
    hid = w_first.shape[1]
    tile_row = tile_ids.reshape(1, samples)
    grid_table = lax.all_gather(grid, "dp", axis=0, tiled=True)

    send_info, rank = pl.pallas_call(
        functools.partial(slot_kernel, tiles=owners, capacity=capacity),
        out_shape=[
            jax.ShapeDtypeStruct((FIELDS, owners, capacity), bf16),
            jax.ShapeDtypeStruct((1, samples), f32),
        ],
    )(tile_row, corners, offsets)
    info = from_peers(to_peers(send_info), FIELDS).reshape(FIELDS, slot_count)
    info = jnp.pad(info, ((0, 16 - FIELDS), (0, 0)))

    first_t = w_first.T
    second_8 = jnp.pad(w_second, ((0, 0), (0, 4)))
    features, hidden, slope, decoded = forward_call(
        info, grid_table, first_t, jnp.pad(second_8, ((0, 0), (0, 8))).T
    )

    back = from_peers(to_peers(decoded[0:4].reshape(4, owners, capacity)), 4)
    send_grads = pl.pallas_call(
        functools.partial(shade_kernel, tiles=owners, capacity=capacity),
        out_shape=jax.ShapeDtypeStruct((4, owners, capacity), f32),
    )(tile_row, rank, back, targets)
    grads = from_peers(to_peers(send_grads), 4).reshape(4, slot_count)
    grads = jnp.pad(grads, ((0, 4), (0, 0)))

    second_24 = jnp.concatenate([second_8] * 3, axis=1)
    feature_grad, grad_first, grad_second = backward_call(
        grads, hidden, slope, features, w_first, second_24
    )
    full_grad = spread_call(info, feature_grad, cells)
    grid_grad = lax.psum_scatter(full_grad, "dp", scatter_dimension=0, tiled=True)
    grad_first, grad_second = all_sum(grad_first, grad_second[0:4])
    return (grid_grad, grad_first, grad_second)


def solution(mesh):
    in_specs = (
        P(("tile", "dp"), None),
        P(None, ("tile", "dp")),
        P(None, ("tile", "dp")),
        P(None, ("tile", "dp")),
        P("dp", "tile"),
        P(),
        P(),
    )
    out_specs = (P("dp", "tile"), P(), P())
    return jax.shard_map(body, mesh=mesh, in_specs=in_specs, out_specs=out_specs, check_vma=False)
```

time: 585 us -> 211 us (0.36)
  other arithmetic: 161 us -> 1.95 us
  waiting for transfers between devices: 165 us -> 32.6 us
  local copies, waits for them, and re-layouts: 103 us -> 14.7 us
  Pallas kernels: 0 us -> 43.1 us
  blocking collectives: 99 us -> 84 us
  starting transfers between devices: 32.5 us -> 19.5 us
  matrix products: 8.76 us -> 0 us
    scatter-add x4 -> x0, other arithmetic: 130 us -> none  [spread(): total.at[corner_cells[corner]]]
    psum x1 -> x0, blocking collectives: 99 us -> none  [body(): lax.psum((grad_first, grad_second), ('tile', 'dp'))]
    all_to_all x4 -> x2, waiting for transfers between devices: 111 us -> 15.6 us  [over_tile(): return lax.all_to_all(x, 'tile', split_axis=0, concat_axis=0, tiled=True)]
    all_to_all x0 -> x4, blocking collectives: none -> 84 us  [the longest x3 71.3 us: over_tile(): return lax.all_to_all(x, 'tile', split_axis=0, concat_axis=0, tiled=True)]
    gather x5 -> x0, local copies, waits for them, and re-layouts: 71.6 us -> none  [the longest x4 67.7 us: interpolate(): picked = cell_rows[corner_cells[corner]].astype(jnp.float32)]
    unnamed x4 -> x2, waiting for transfers between devices: 53.7 us -> 0.7 us
    pallas_call x0 -> x5, Pallas kernels: none -> 43.1 us  [the longest x1 15.6 us: forward_call(): pl.pallas_call(forward_kernel, grid=(slots // block,), in_specs=[pl.Block...]
    another operation x5 -> x0, other arithmetic: 19 us -> none
  transfers between devices with their start and end apart: 7 -> 4, of which waited for: 5 -> 3; matrix products, arithmetic and copies ran while one was open for 30% -> 5% of each run, Pallas kernels for 0% -> 1%
where the time goes in v1:
time: 211 us; the launch traced here: 210 us
  blocking collectives  84 us (40%)
  Pallas kernels  43.1 us (20%)
  waiting for transfers between devices  32.6 us (15%)
  starting transfers between devices  19.5 us (9%)
  local copies, waits for them, and re-layouts  14.7 us (7%)
  between operations  14.2 us (7%)
    all_to_all x3, blocking collectives, over_tile(): return lax.all_to_all(x, 'tile', split_axis=0, concat_axis=0, tiled=True)  71.3 us
    all_to_all x2, starting transfers between devices, over_tile(): return lax.all_to_all(x, 'tile', split_axis=0, concat_axis=0, tiled=True)  19.3 us
    all_gather x1, waiting for transfers between devices, body(): grid_table = lax.all_gather(grid, 'dp', axis=0, tiled=True)  16.3 us
    all_to_all x2, waiting for transfers between devices, over_tile(): return lax.all_to_all(x, 'tile', split_axis=0, concat_axis=0, tiled=True)  15.6 us
    pallas_call x1, Pallas kernels, forward_call(): pl.pallas_call(forward_kernel, grid=(slots // block,), in_specs=[pl.Block...  15.6 us
    all_to_all x1, blocking collectives, all_sum(): lax.all_to_all(copies, 'dp', split_axis=0, concat_axis=0, tiled=True)  12.7 us
    pallas_call x1, Pallas kernels, spread_call(): pl.pallas_call(functools.partial(spread_kernel, cell_block=cell_block, sl...  12.2 us
    pallas_call x1, Pallas kernels, backward_call(): pl.pallas_call(backward_kernel, grid=(slots // block,), in_specs=[pl.Bloc...  8.91 us
  transfers between devices with their start and end apart: 4, of which 3 were waited for; matrix products, arithmetic and copies ran while one was open for 5% of the time, Pallas kernels for 1%

profile of v1, /device:TPU:1, one launch (start us, length us, event | category | flops | bytes accessed | tf_op | source)
XLA Modules:
  0.0 210.1 jit_solution(2462585187147639409)
XLA Ops:
  7.2 0.0 all-gather.2.cloned.1.call-start
  7.2 0.7 all-gather.2.cloned.1.call-update
  7.9 2.1 shard_map.94
  10.0 1.0 copy.44
  10.9 0.1 all_to_all.45
  11.1 0.5 broadcast.17
  11.6 0.9 reduce.5
  12.5 0.7 reshape.82
  13.2 14.8 %all-to-all-start = ((bf16[64,2,192]{2,1,0:T(2,128)(2,1)}), bf16[64,2,192]{2,1,0:T(2,128)(2,1)S(1)}, u32[]{:S(2)}, u32[]{:S(2)}) async-start(bf16[64,2,192]{2,1,0:T(2,128)(2,1)} %reshape.82), calls=%async_computation | async-start | bytes 131072 | tf_op jit(solution)/shard_map/all_to_all | solution.py:243
  28.1 1.8 copy.47
  29.9 0.7 pad.17
  30.6 0.6 pad_bitcast_fusion.second_t_ref
  31.2 6.7 %all-to-all-done = bf16[64,2,192]{2,1,0:T(2,128)(2,1)S(1)} async-done(((bf16[64,2,192]{2,1,0:T(2,128)(2,1)}), bf16[64,2,192]{2,1,0:T(2,128)(2,1)S(1)}, u32[]{:S(2)}, u32[]{:S(2)}) %all-to-all-start) | async-done | bytes 49184 | tf_op jit(solution)/shard_map/all_to_all | solution.py:243
  37.9 0.1 reshape.83
  38.0 0.3 reduce.2
  38.3 0.1 reshape.69
  38.4 0.1 reshape.70
  38.6 0.7 pad.16.info_ref
  39.2 16.3 %all-gather.2.cloned.1.call-done.grid_ref = bf16[256,4096]{1,0:T(8,128)(2,1)} async-done(((bf16[32,4096]{1,0:T(8,128)(2,1)}), bf16[256,4096]{1,0:T(8,128)(2,1)}) %all-gather.2.cloned.1.call-update) | async-done | bytes 2097168 | tf_op jit(solution)/shard_map/all_gather | solution.py:280
  55.5 15.6 %shard_map.95 = (bf16[256,4096]{1,0:T(8,128)(2,1)}, bf16[512,4096]{1,0:T(8,128)(2,1)}, f32[512,4096]{1,0:T(8,128)}, f32[8,4096]{1,0:T(8,128)}) custom-call(bf16[16,4096]{1,0:T(8,128)(2,1)} %pad.16.info_ref, bf16[256,4096]{1,0:T(8,128)(2,1)} %all-gather.2.cloned.1.call-done.grid_ref, bf16[512,256]{1,0:T(8,128)(2,1)} %bitcast.20, ...), custom_call_target="tpu_custom_call" | custom-call | tf_op jit(solution)/shard_map/pallas_call | solution.py:101
  71.1 0.9 slice.12
  72.0 0.1 reshape.71
  72.1 0.1 copy.63
  72.2 0.1 all_to_all.46
  72.4 24.3 %all_to_all.54 = f32[64,1,256]{2,1,0:T(1,128)S(1)} all-to-all(f32[64,1,256]{2,1,0:T(1,128)S(1)} %all_to_all.46), channel_id=1, replica_groups=mesh['tile'=64,'dp'=8] {'tile'}, dimensions={0} | all-to-all | bytes 131072 | tf_op jit(solution)/shard_map/all_to_all | solution.py:243
  96.6 0.2 reduce.3
  96.8 0.1 reshape.72
  96.9 0.7 copy.62
  97.6 4.3 %shard_map.96 = f32[4,64,64]{2,1,0:T(8,128)} custom-call(s32[1,1024]{1,0:T(1,128)} %bitcast.28, f32[1,1024]{1,0:T(1,128)} %get-tuple-element.13.rank_ref, f32[4,64,64]{2,1,0:T(8,128)} %bitcast.22, f32[3,64]{1,0:T(4,128)} %targets_ref.1), custom_call_target="tpu_custom_call" | custom-call | tf_op jit(solution)/shard_map/pallas_call | solution.py:299
  101.9 1.0 copy.51
  102.9 0.8 all_to_all.47
  103.6 4.4 %all-to-all-start.2 = ((f32[64,1,256]{2,1,0:T(1,128)}), f32[64,1,256]{2,1,0:T(1,128)S(1)}, u32[]{:S(2)}, u32[]{:S(2)}) async-start(f32[64,1,256]{2,1,0:T(1,128)} %all_to_all.47), calls=%async_computation.2 | async-start | bytes 131072 | tf_op jit(solution)/shard_map/all_to_all | solution.py:243
  108.1 0.2 reduce-scatter.2.cloned.1.call-start
  108.3 0.8 copy.54.second_ref
  109.1 8.9 %all-to-all-done.2 = f32[64,1,256]{2,1,0:T(1,128)S(1)} async-done(((f32[64,1,256]{2,1,0:T(1,128)}), f32[64,1,256]{2,1,0:T(1,128)S(1)}, u32[]{:S(2)}, u32[]{:S(2)}) %all-to-all-start.2) | async-done | bytes 65568 | tf_op jit(solution)/shard_map/all_to_all | solution.py:243
  118.0 0.2 reduce.4
  118.1 0.1 reshape.73
  118.3 0.1 reshape.74
  118.4 0.7 pad.19.grads_ref
  119.1 8.9 %shard_map.97 = (bf16[256,4096]{1,0:T(8,128)(2,1)}, f32[256,512]{1,0:T(8,128)}, f32[8,512]{1,0:T(8,128)}) custom-call(f32[8,4096]{1,0:T(8,128)} %pad.19.grads_ref, bf16[512,4096]{1,0:T(8,128)(2,1)} %get-tuple-element.15.hidden_ref, f32[512,4096]{1,0:T(8,128)} %get-tuple-element.16.slope_ref, bf16[256,4096]{1,0:T(8,128)(2,1)} %get-tuple-element.17.features_ref, ...), custom_call_target="tpu_custom_call" | custom-call | tf_op jit(solution)/shard_map/pallas_call | solution.py:193
  128.0 0.0 copy-start.1
  128.0 0.0 copy-start
  128.0 12.2 %shard_map.98 = f32[256,4096]{1,0:T(8,128)} custom-call(bf16[16,4096]{1,0:T(8,128)(2,1)} %pad.16.info_ref, bf16[256,4096]{1,0:T(8,128)(2,1)} %get-tuple-element.18.grads_ref), custom_call_target="tpu_custom_call" | custom-call | tf_op jit(solution)/shard_map/pallas_call | solution.py:231
  140.2 0.0 reduce-scatter.2.cloned.1.call-update
  140.2 0.0 copy-done.1
  140.3 0.1 reshape.76
  140.3 0.0 copy-done
  140.3 0.2 reshape.75
  140.6 0.4 all_to_all.40
  141.0 21.9 %all_to_all.55 = f32[64,1,2080]{2,1,0:T(1,128)S(1)} all-to-all(f32[64,1,2080]{2,1,0:T(1,128)S(1)} %all_to_all.40), channel_id=1, replica_groups=mesh['tile'=64,'dp'=8] {'tile'}, dimensions={0} | all-to-all | bytes 1064960 | tf_op jit(solution)/shard_map/all_to_all | solution.py:243
  162.9 0.4 reduce_sum.18
  163.3 12.7 %all_to_all.56 = f32[8,1,2080]{2,1,0:T(1,128)S(1)} all-to-all(f32[8,1,2080]{2,1,0:T(1,128)S(1)} %broadcast_in_dim.4), channel_id=1, replica_groups=mesh['tile'=64,'dp'=8] {'dp'}, dimensions={0} | all-to-all | bytes 133120 | tf_op jit(solution)/shard_map/all_to_all | solution.py:264
  176.0 0.1 reduce_sum.19
  176.1 0.3 broadcast_in_dim.5
  176.4 25.2 %all_to_all.57 = f32[64,1,2080]{2,1,0:T(1,128)S(1)} all-to-all(f32[64,1,2080]{2,1,0:T(1,128)S(1)} %broadcast_in_dim.5), channel_id=1, replica_groups=mesh['tile'=64,'dp'=8] {'tile'}, dimensions={0} | all-to-all | bytes 1064960 | tf_op jit(solution)/shard_map/all_to_all | solution.py:243
  201.6 0.7 reshape.78
  202.3 0.9 reshape.77
  203.3 0.0 reduce-scatter.2.cloned.1.call-done
  (9 shorter events, 0.2 us)
Async XLA Ops:
  7.2 48.3 %all-gather.2.cloned.1.call-start = ((), (), s32[]{:S(2)}) async-start(), calls=%async_computation.7 | async-start | bytes 2359296 | tf_op jit(solution)/shard_map/all_gather | solution.py:280
  13.2 24.6 %all-to-all-start = ((bf16[64,2,192]{2,1,0:T(2,128)(2,1)}), bf16[64,2,192]{2,1,0:T(2,128)(2,1)S(1)}, u32[]{:S(2)}, u32[]{:S(2)}) async-start(bf16[64,2,192]{2,1,0:T(2,128)(2,1)} %reshape.82), calls=%async_computation | async-start | bytes 131072 | tf_op jit(solution)/shard_map/all_to_all | solution.py:243
  103.6 14.3 %all-to-all-start.2 = ((f32[64,1,256]{2,1,0:T(1,128)}), f32[64,1,256]{2,1,0:T(1,128)S(1)}, u32[]{:S(2)}, u32[]{:S(2)}) async-start(f32[64,1,256]{2,1,0:T(1,128)} %all_to_all.47), calls=%async_computation.2 | async-start | bytes 131072 | tf_op jit(solution)/shard_map/all_to_all | solution.py:243
  108.1 95.2 %reduce-scatter.2.cloned.1.call-start = ((), (), s32[]{:S(2)}) async-start(), calls=%async_computation.8 | async-start | bytes 4718592 | tf_op jit(solution)/shard_map/reduce_scatter | solution.py:311
  128.0 12.3 %copy-start.1 = (f32[8,512]{1,0:T(8,128)S(1)}, f32[8,512]{1,0:T(8,128)}, u32[]{:S(2)}) copy-start(f32[8,512]{1,0:T(8,128)} %get-tuple-element.20) | copy-start | bytes 49156
  128.0 12.4 %copy-start = (f32[256,512]{1,0:T(8,128)S(1)}, f32[256,512]{1,0:T(8,128)}, u32[]{:S(2)}) copy-start(f32[256,512]{1,0:T(8,128)} %get-tuple-element.19) | copy-start | bytes 1572868
Sparse Core Ops, SparseCore 0:
  10.1 45.3 all-gather.1
  140.4 51.3 reduce-scatter.1

commit v2 on v1

v2 whole, which is shorter than its diff:
```python
import functools

import jax
import jax.numpy as jnp
from jax import lax
from jax.experimental import pallas as pl
from jax.experimental.pallas import tpu as pltpu
from jax.sharding import PartitionSpec as P

GSIDE = 64
MARCH = 15
march_step = 0.1
ambient = 0.3

bf16 = jnp.bfloat16
f32 = jnp.float32
HIGHEST = lax.Precision.HIGHEST
FIELDS = 6
VMEM_BYTES = 56 << 20
SMALL_VMEM_BYTES = 12 << 20


def matmul(a, b, dims=((1,), (0,)), precision=None):
    return lax.dot_general(a, b, (dims, ((), ())), precision=precision, preferred_element_type=f32)


def row_iota(shape, dim):
    return lax.broadcasted_iota(jnp.int32, shape, dim)


def slot_kernel(tile_ref, corners_ref, offsets_ref, send_ref, rank_ref, *, tiles, capacity):
    tile = tile_ref[...]
    samples = tile.shape[1]
    members = row_iota((tiles, samples), 0) == tile
    member_rows = members.astype(f32).astype(bf16)
    before = (
        row_iota((samples, samples), 0) < row_iota((samples, samples), 1)
    ).astype(f32).astype(bf16)
    earlier = matmul(member_rows, before)
    rank = jnp.sum(jnp.where(members, earlier, 0.0), axis=0, keepdims=True)
    rank_ref[...] = rank
    at_rank = row_iota((capacity, samples), 0) == rank.astype(jnp.int32)
    along = offsets_ref[0:1]
    across = offsets_ref[1:2]
    fields = [
        corners_ref[0:1].astype(f32),
        corners_ref[1:2].astype(f32),
        (1.0 - along) * (1.0 - across),
        (1.0 - along) * across,
        along * (1.0 - across),
        along * across,
    ]
    for pair in range(FIELDS // 2):
        placed = jnp.concatenate(
            [jnp.where(at_rank, field, 0.0) for field in fields[2 * pair : 2 * pair + 2]], axis=0
        )
        send_ref[:, pair, :] = matmul(member_rows, placed.astype(bf16), ((1,), (1,)))
    send_ref[:, FIELDS // 2, :] = jnp.zeros((tiles, 2 * capacity), f32)


def sample_columns(info):
    slots = info.shape[1]
    col = row_iota((GSIDE, slots), 0).astype(f32).astype(bf16)

    def full(number):
        return jnp.broadcast_to(info[number : number + 1], (GSIDE, slots))

    zero = jnp.zeros((GSIDE, slots), bf16)
    here = col == full(1)
    after = col == full(1) + jnp.ones((), bf16)
    upper = jnp.where(here, full(2), jnp.where(after, full(3), zero))
    lower = jnp.where(here, full(4), jnp.where(after, full(5), zero))
    return full(0), upper, lower


def weight_rows(row, upper, lower, count):
    zero = jnp.zeros_like(upper)
    for a in range(count):
        yield a, jnp.where(row == float(a), upper, jnp.where(row == float(a - 1), lower, zero))


def logistic(x):
    return 0.5 + 0.5 * jnp.tanh(0.5 * x)


def forward_kernel(
    info_ref, grid_ref, first_t_ref, second_t_ref, features_ref, decoded_ref, weights_ref, *, rows
):
    row, upper, lower = sample_columns(info_ref[...].astype(bf16))
    cells = rows * GSIDE
    total = None
    for first_row in range(0, GSIDE, rows):
        here = pl.ds(first_row * GSIDE, cells)
        for a, piece in weight_rows(row - float(first_row), upper, lower, rows):
            weights_ref[pl.ds((first_row + a) * GSIDE, GSIDE), :] = piece
        term = matmul(grid_ref[:, here], weights_ref[here, :])
        total = term if total is None else total + term
    features = total.astype(bf16)
    features_ref[...] = features
    pre_act = matmul(first_t_ref[...], features)
    hidden = (pre_act * logistic(pre_act)).astype(bf16)
    decoded_ref[...] = matmul(second_t_ref[...], hidden)[0:4]


def forward_call(info, grid_table, first_t, second_t, block=1024, rows=8):
    channels, cells = grid_table.shape
    hid = first_t.shape[0]
    slots = info.shape[1]
    whole = lambda s: (0, 0)
    part = lambda s: (0, s)
    return pl.pallas_call(
        functools.partial(forward_kernel, rows=rows),
        grid=(slots // block,),
        in_specs=[
            pl.BlockSpec((8, block), part),
            pl.BlockSpec((channels, cells), whole),
            pl.BlockSpec((hid, channels), whole),
            pl.BlockSpec((16, hid), whole),
        ],
        out_specs=[pl.BlockSpec((channels, block), part), pl.BlockSpec((4, block), part)],
        out_shape=[
            jax.ShapeDtypeStruct((channels, slots), bf16),
            jax.ShapeDtypeStruct((4, slots), f32),
        ],
        scratch_shapes=[pltpu.VMEM((cells, block), bf16)],
        compiler_params=pltpu.CompilerParams(vmem_limit_bytes=VMEM_BYTES),
    )(info, grid_table, first_t, second_t)


def shade_kernel(tile_ref, rank_ref, back_ref, targets_ref, send_ref, *, tiles, capacity):
    tile = tile_ref[...]
    samples = tile.shape[1]
    rays = targets_ref.shape[1]
    members = (row_iota((tiles, samples), 0) == tile).astype(f32)
    at_rank = row_iota((capacity, samples), 0) == rank_ref[...].astype(jnp.int32)
    decoded = []
    for number in range(4):
        spread = matmul(
            back_ref[:, number * capacity : (number + 1) * capacity], members, ((0,), (0,)), HIGHEST
        )
        decoded.append(jnp.sum(jnp.where(at_rank, spread, 0.0), axis=0, keepdims=True))
    raw = decoded[0]
    ray_of = row_iota((rays, samples), 1) // (MARCH + 1) == row_iota((rays, samples), 0)
    first = row_iota((rays, samples), 1) == row_iota((rays, samples), 0) * (MARCH + 1)
    on_march = jnp.where(ray_of & ~first, 1.0, 0.0)
    on_surface = jnp.where(first, 1.0, 0.0)
    density = jnp.maximum(raw, 0.0) + jnp.log1p(jnp.exp(-jnp.abs(raw)))
    along_rays = ((1,), (1,))
    total = matmul(jnp.broadcast_to(density, (8, samples)), on_march, along_rays, HIGHEST)[0:1]
    colours = jnp.concatenate(decoded[1:] + [jnp.zeros((5, samples), f32)], axis=0)
    surface = matmul(colours, on_surface, along_rays, HIGHEST)
    transmit = jnp.exp(-march_step * total)
    lighting = ambient + (1.0 - ambient) * transmit
    albedo = jax.nn.sigmoid(surface[0:3])
    errors = albedo * lighting - targets_ref[...]
    surface_grad = errors * lighting * albedo * (1.0 - albedo)
    transmit_grad = (1.0 - ambient) * jnp.sum(errors * albedo, axis=0, keepdims=True)
    march_grad = -march_step * transmit * transmit_grad
    march_all = matmul(jnp.broadcast_to(march_grad, (8, rays)), on_march, precision=HIGHEST)[0:1]
    surface_all = matmul(
        jnp.concatenate([surface_grad, jnp.zeros((5, rays), f32)], axis=0),
        on_surface,
        precision=HIGHEST,
    )
    grads = [march_all * jax.nn.sigmoid(raw)] + [surface_all[k : k + 1] for k in range(3)]
    for number in range(4):
        placed = jnp.where(at_rank, grads[number], 0.0)
        send_ref[:, number * capacity : (number + 1) * capacity] = matmul(
            members, placed, along_rays, HIGHEST
        )


def exact_pieces(grads):
    grads = jnp.concatenate([grads, jnp.zeros_like(grads)], axis=0)
    high = grads.astype(bf16).astype(f32)
    rest = grads - high
    mid = rest.astype(bf16).astype(f32)
    return jnp.concatenate([high, mid, rest - mid], axis=0).astype(bf16)


def exact_pieces(grads):
    grads = jnp.concatenate([grads, jnp.zeros_like(grads)], axis=0)
    high = grads.astype(bf16).astype(f32)
    rest = grads - high
    mid = rest.astype(bf16).astype(f32)
    return jnp.concatenate([high, mid, rest - mid], axis=0).astype(bf16)


def backward_kernel(
    grads_ref, features_ref, first_t_ref, first_ref, second_ref,
    feature_grad_ref, grad_first_ref, grad_second_ref, first_sum, second_sum,
):
    @pl.when(pl.program_id(0) == 0)
    def _():
        first_sum[...] = jnp.zeros_like(first_sum)
        second_sum[...] = jnp.zeros_like(second_sum)

    features = features_ref[...]
    pre_act = matmul(first_t_ref[...], features)
    gate = logistic(pre_act)
    hidden = (pre_act * gate).astype(bf16)
    pieces = exact_pieces(grads_ref[...])
    hidden_grad = matmul(second_ref[...], pieces)
    pre_grad = (hidden_grad * gate * (1.0 + pre_act * (1.0 - gate))).astype(bf16)
    feature_grad_ref[...] = matmul(first_ref[...], pre_grad).astype(bf16)
    first_sum[...] += matmul(features, pre_grad, ((1,), (1,)))
    second_sum[...] += matmul(pieces, hidden, ((1,), (1,)))

    @pl.when(pl.program_id(0) == pl.num_programs(0) - 1)
    def _():
        grad_first_ref[...] = first_sum[...].astype(bf16)
        grad_second_ref[...] = (second_sum[0:8] + second_sum[8:16] + second_sum[16:24])[0:4]


def backward_call(grads, features, first_t, first, second, block=1024):
    hid, channels = first_t.shape
    slots = grads.shape[1]
    whole = lambda s: (0, 0)
    part = lambda s: (0, s)
    return pl.pallas_call(
        backward_kernel,
        grid=(slots // block,),
        in_specs=[
            pl.BlockSpec((4, block), part),
            pl.BlockSpec((channels, block), part),
            pl.BlockSpec((hid, channels), whole),
            pl.BlockSpec((channels, hid), whole),
            pl.BlockSpec((hid, 24), whole),
        ],
        out_specs=[
            pl.BlockSpec((channels, block), part),
            pl.BlockSpec((channels, hid), whole),
            pl.BlockSpec((4, hid), whole),
        ],
        out_shape=[
            jax.ShapeDtypeStruct((channels, slots), bf16),
            jax.ShapeDtypeStruct((channels, hid), bf16),
            jax.ShapeDtypeStruct((4, hid), f32),
        ],
        scratch_shapes=[pltpu.VMEM((channels, hid), f32), pltpu.VMEM((24, hid), f32)],
        compiler_params=pltpu.CompilerParams(vmem_limit_bytes=VMEM_BYTES),
    )(grads, features, first_t, first, second)


def spread_kernel(info_ref, grads_ref, out_ref, weights_ref, *, slot_block):
    rows = out_ref.shape[1] // GSIDE
    start = jnp.full((1, 1), pl.program_id(0) * rows, jnp.int32).astype(f32).astype(bf16)
    total = None
    for s in range(0, info_ref.shape[1], slot_block):
        here = slice(s, s + slot_block)
        row, upper, lower = sample_columns(info_ref[:, here].astype(bf16))
        for a, piece in weight_rows(row - start, upper, lower, rows):
            weights_ref[pl.ds(a * GSIDE, GSIDE), here] = piece
        term = matmul(grads_ref[:, here], weights_ref[:, here], ((1,), (1,)))
        total = term if total is None else total + term
    out_ref[...] = total


def spread_call(info, grads, cells, block=1024, slot_block=512):
    channels, slots = grads.shape
    whole = lambda s: (0, 0)
    return pl.pallas_call(
        functools.partial(spread_kernel, slot_block=slot_block),
        grid=(cells // block,),
        in_specs=[pl.BlockSpec((8, slots), whole), pl.BlockSpec((channels, slots), whole)],
        out_specs=pl.BlockSpec((channels, block), lambda s: (0, s)),
        out_shape=jax.ShapeDtypeStruct((channels, cells), f32),
        scratch_shapes=[pltpu.VMEM((block, slots), bf16)],
        compiler_params=pltpu.CompilerParams(vmem_limit_bytes=VMEM_BYTES),
    )(info, grads)


def over_tile(x):
    return lax.all_to_all(x, "tile", split_axis=0, concat_axis=0, tiled=True)


def all_sum(grad_first, grad_second):
    owners = lax.axis_size("tile")
    groups = lax.axis_size("dp")
    channels, hid = grad_first.shape
    first = grad_first.reshape(owners, channels // owners, hid)
    second = grad_second.astype(bf16).reshape(4, owners, hid // owners).transpose(1, 0, 2)
    second = jnp.pad(second, ((0, 0), (0, 0), (0, 128 - hid // owners)))
    mine = jnp.sum(over_tile(jnp.concatenate([first, second], axis=2)).astype(f32), axis=0)
    copies = jnp.broadcast_to(mine, (groups,) + mine.shape)
    shared = lax.all_to_all(copies, "dp", split_axis=0, concat_axis=0, tiled=True)
    summed = jnp.sum(shared, axis=0).astype(bf16)
    everything = over_tile(jnp.broadcast_to(summed, (owners,) + summed.shape)).astype(f32)
    first = everything[:, :, :hid].reshape(channels, hid)
    second = everything[:, :, hid : hid + hid // owners].transpose(0, 2, 1).reshape(hid, 4)
    return first, second


def body(tile_ids, corners, offsets, targets, grid, w_first, w_second):
    owners = lax.axis_size("tile")
    samples = tile_ids.shape[0]
    capacity = 4 * samples // owners
    slot_count = owners * capacity
    cells = grid.shape[1]
    tile_row = tile_ids.reshape(1, samples)
    grid_table = lax.all_gather(grid, "dp", axis=0, tiled=True)

    send_info, rank = pl.pallas_call(
        functools.partial(slot_kernel, tiles=owners, capacity=capacity),
        out_shape=[
            jax.ShapeDtypeStruct((owners, FIELDS // 2 + 1, 2 * capacity), f32),
            jax.ShapeDtypeStruct((1, samples), f32),
        ],
        compiler_params=pltpu.CompilerParams(vmem_limit_bytes=SMALL_VMEM_BYTES),
    )(tile_row, corners, offsets)
    first_t = w_first.T
    second_8 = jnp.pad(w_second, ((0, 0), (0, 4)))
    second_t = jnp.pad(second_8, ((0, 0), (0, 8))).T
    info = over_tile(send_info).reshape(owners, 8, capacity).transpose(1, 0, 2)
    info = info.reshape(8, slot_count)

    features, decoded = forward_call(info, grid_table, first_t, second_t)

    back = over_tile(decoded.reshape(4, owners, capacity).transpose(1, 0, 2).reshape(owners, 2, -1))
    send_grads = pl.pallas_call(
        functools.partial(shade_kernel, tiles=owners, capacity=capacity),
        out_shape=jax.ShapeDtypeStruct((owners, 4 * capacity), f32),
        compiler_params=pltpu.CompilerParams(vmem_limit_bytes=SMALL_VMEM_BYTES),
    )(tile_row, rank, back.reshape(owners, 4 * capacity), targets)
    grads = over_tile(send_grads.reshape(owners, 2, -1))
    grads = grads.reshape(owners, 4, capacity).transpose(1, 0, 2).reshape(4, slot_count)

    second_24 = jnp.concatenate([second_8] * 3, axis=1)
    feature_grad, grad_first, grad_second = backward_call(
        grads, features, first_t, w_first, second_24
    )
    share = spread_call(info, feature_grad, cells)
    grid_grad = lax.psum_scatter(share, "dp", scatter_dimension=0, tiled=True)
    share, grad_first, grad_second = lax.optimization_barrier((share, grad_first, grad_second))
    grad_first, grad_second = all_sum(grad_first, grad_second)
    return (grid_grad, grad_first, grad_second)


def solution(mesh):
    in_specs = (
        P(("tile", "dp"), None),
        P(None, ("tile", "dp")),
        P(None, ("tile", "dp")),
        P(None, ("tile", "dp")),
        P("dp", "tile"),
        P(),
        P(),
    )
    out_specs = (P("dp", "tile"), P(), P())
    return jax.shard_map(body, mesh=mesh, in_specs=in_specs, out_specs=out_specs, check_vma=False)
```

time: 211 us -> 197 us (0.934)
  blocking collectives: 84 us -> 74.7 us
  Pallas kernels: 43.1 us -> 39.7 us
    all_to_all x3, blocking collectives: 71.3 us -> 61.6 us  [over_tile(): return lax.all_to_all(x, 'tile', split_axis=0, concat_axis=0, tiled=True)]
    unnamed x8 -> x17, local copies, waits for them, and re-layouts: 2.71 us -> 4.87 us
  transfers between devices with their start and end apart: 4 -> 4, of which waited for: 3 -> 3; matrix products, arithmetic and copies ran while one was open for 5% -> 4% of each run, Pallas kernels for 1% -> 1%
where the time goes in v2:
time: 197 us; the launch traced here: 196 us
  blocking collectives  74.7 us (38%)
  Pallas kernels  39.7 us (20%)
  waiting for transfers between devices  34.7 us (18%)
  starting transfers between devices  19.5 us (10%)
  between operations  14.2 us (7%)
  local copies, waits for them, and re-layouts  12.6 us (6%)
    all_to_all x3, blocking collectives, over_tile(): return lax.all_to_all(x, 'tile', split_axis=0, concat_axis=0, tiled=True)  61.6 us
    all_to_all x2, starting transfers between devices, over_tile(): return lax.all_to_all(x, 'tile', split_axis=0, concat_axis=0, tiled=True)  19.3 us
    all_gather x1, waiting for transfers between devices, body(): grid_table = lax.all_gather(grid, 'dp', axis=0, tiled=True)  17.9 us
    all_to_all x2, waiting for transfers between devices, over_tile(): return lax.all_to_all(x, 'tile', split_axis=0, concat_axis=0, tiled=True)  16.2 us
    pallas_call x1, Pallas kernels, forward_call(): pl.pallas_call(functools.partial(forward_kernel, rows=rows), grid=(slots...  13.8 us
    all_to_all x1, blocking collectives, all_sum(): lax.all_to_all(copies, 'dp', split_axis=0, concat_axis=0, tiled=True)  13.1 us
    pallas_call x1, Pallas kernels, spread_call(): pl.pallas_call(functools.partial(spread_kernel, slot_block=slot_block), g...  12.2 us
    pallas_call x1, Pallas kernels, backward_call(): pl.pallas_call(backward_kernel, grid=(slots // block,), in_specs=[pl.Bloc...  9.4 us
  transfers between devices with their start and end apart: 4, of which 3 were waited for; matrix products, arithmetic and copies ran while one was open for 4% of the time, Pallas kernels for 1%

profile of v2, /device:TPU:1, one launch (start us, length us, event | category | flops | bytes accessed | tf_op | source)
XLA Modules:
  0.0 196.0 jit_solution(10523385668858887265)
XLA Ops:
  7.2 0.0 all-gather.2.cloned.1.call-start
  7.2 0.7 all-gather.2.cloned.1.call-update
  7.9 0.0 copy-start
  7.9 0.7 copy-done
  8.6 0.0 copy-start.2
  8.6 0.7 copy-done.2
  9.3 0.0 copy-start.3
  9.3 0.7 copy-done.3
  10.0 1.5 shard_map.94
  11.5 14.8 %all-to-all-start = ((f32[64,4,128]{2,1,0:T(4,128)}), f32[64,4,128]{2,1,0:T(4,128)S(1)}, u32[]{:S(2)}, u32[]{:S(2)}) async-start(f32[64,4,128]{2,1,0:T(4,128)} %get-tuple-element.12), calls=%async_computation | async-start | bytes 262144 | tf_op jit(solution)/shard_map/all_to_all | solution.py:274
  26.3 1.8 copy.40
  28.1 0.7 pad.12
  28.8 0.6 pad_bitcast_fusion.second_t_ref
  29.4 7.3 %all-to-all-done = f32[64,4,128]{2,1,0:T(4,128)S(1)} async-done(((f32[64,4,128]{2,1,0:T(4,128)}), f32[64,4,128]{2,1,0:T(4,128)S(1)}, u32[]{:S(2)}, u32[]{:S(2)}) %all-to-all-start) | async-done | bytes 131104 | tf_op jit(solution)/shard_map/all_to_all | solution.py:274
  36.7 0.1 reshape.46
  36.8 0.0 copy-start.1
  36.8 0.0 copy-start.4
  36.8 0.1 copy.52
  36.9 0.8 reshape.47.info_ref
  37.6 17.9 %all-gather.2.cloned.1.call-done.grid_ref = bf16[256,4096]{1,0:T(8,128)(2,1)} async-done(((bf16[32,4096]{1,0:T(8,128)(2,1)}), bf16[256,4096]{1,0:T(8,128)(2,1)}) %all-gather.2.cloned.1.call-update) | async-done | bytes 2097168 | tf_op jit(solution)/shard_map/all_gather | solution.py:301
  55.5 13.8 %shard_map.95 = (bf16[256,4096]{1,0:T(8,128)(2,1)}, f32[4,4096]{1,0:T(4,128)}) custom-call(f32[8,4096]{1,0:T(8,128)} %reshape.47.info_ref, bf16[256,4096]{1,0:T(8,128)(2,1)} %all-gather.2.cloned.1.call-done.grid_ref, bf16[512,256]{1,0:T(8,128)(2,1)} %bitcast.21, bf16[16,512]{1,0:T(8,128)(2,1)} %pad_bitcast_fusion.second_t_ref), custom_call_target="tpu_custom_call" | custom-call | tf_op jit(solution)/shard_map/pallas_call | solution.py:111
  69.3 1.0 reshape.48
  70.3 0.1 copy.41
  70.4 0.1 reshape.49
  70.5 24.2 %all_to_all.30 = f32[64,2,128]{2,1,0:T(2,128)S(1)} all-to-all(f32[64,2,128]{2,1,0:T(2,128)S(1)} %reshape.49), channel_id=1, replica_groups=mesh['tile'=64,'dp'=8] {'tile'}, dimensions={0} | all-to-all | bytes 131072 | tf_op jit(solution)/shard_map/all_to_all | solution.py:274
  94.8 0.0 copy-done.1
  94.8 0.0 copy-done.4
  94.8 2.8 %shard_map.96 = f32[64,256]{1,0:T(8,128)S(1)} custom-call(s32[1,1024]{1,0:T(1,128)S(1)} %bitcast.20, f32[1,1024]{1,0:T(1,128)S(1)} %get-tuple-element.13.rank_ref, f32[64,256]{1,0:T(8,128)S(1)} %bitcast.18, f32[3,64]{1,0:T(4,128)S(1)} %copy-done.4), custom_call_target="tpu_custom_call" | custom-call | tf_op jit(solution)/shard_map/pallas_call | solution.py:320
  97.6 0.7 reshape.51
  98.2 4.4 %all-to-all-start.2 = ((f32[64,2,128]{2,1,0:T(2,128)}), f32[64,2,128]{2,1,0:T(2,128)S(1)}, u32[]{:S(2)}, u32[]{:S(2)}) async-start(f32[64,2,128]{2,1,0:T(2,128)} %reshape.51), calls=%async_computation.2 | async-start | bytes 131072 | tf_op jit(solution)/shard_map/all_to_all | solution.py:274
  102.7 0.2 reduce-scatter.2.cloned.1.call-start
  102.9 0.8 copy.43.second_ref
  103.7 8.9 %all-to-all-done.2 = f32[64,2,128]{2,1,0:T(2,128)S(1)} async-done(((f32[64,2,128]{2,1,0:T(2,128)}), f32[64,2,128]{2,1,0:T(2,128)S(1)}, u32[]{:S(2)}, u32[]{:S(2)}) %all-to-all-start.2) | async-done | bytes 65568 | tf_op jit(solution)/shard_map/all_to_all | solution.py:274
  112.6 0.1 reshape.52
  112.8 0.7 reshape.53.grads_ref
  113.5 9.4 %shard_map.97 = (bf16[256,4096]{1,0:T(8,128)(2,1)}, bf16[256,512]{1,0:T(8,128)(2,1)}, f32[4,512]{1,0:T(4,128)}) custom-call(f32[4,4096]{1,0:T(4,128)} %reshape.53.grads_ref, bf16[256,4096]{1,0:T(8,128)(2,1)} %get-tuple-element.15.features_ref, bf16[512,256]{1,0:T(8,128)(2,1)} %bitcast.22, bf16[256,512]{1,0:T(8,128)(2,1)} %first_ref.1, ...), custom_call_target="tpu_custom_call" | custom-call | tf_op jit(solution)/shard_map/pallas_call | solution.py:220
  122.9 12.2 %shard_map.98 = f32[256,4096]{1,0:T(8,128)} custom-call(f32[8,4096]{1,0:T(8,128)} %reshape.47.info_ref, bf16[256,4096]{1,0:T(8,128)(2,1)} %get-tuple-element.16.grads_ref), custom_call_target="tpu_custom_call" | custom-call | tf_op jit(solution)/shard_map/pallas_call | solution.py:262
  135.1 0.0 copy-start.5
  135.1 0.0 copy-start.6
  135.1 0.0 reduce-scatter.2.cloned.1.call-update
  135.1 0.9 copy-done.5
  136.1 0.1 reshape.54
  136.1 0.0 copy-done.6
  136.2 0.1 reshape.55
  136.3 0.1 copy.48
  136.3 0.2 fusion.1
  136.5 17.1 %all_to_all.31 = bf16[64,4,640]{2,1,0:T(4,128)(2,1)S(1)} all-to-all(bf16[64,4,640]{2,1,0:T(4,128)(2,1)S(1)} %fusion.1), channel_id=1, replica_groups=mesh['tile'=64,'dp'=8] {'tile'}, dimensions={0} | all-to-all | bytes 655360 | tf_op jit(solution)/shard_map/all_to_all | solution.py:274
  153.6 0.2 convert_reduce_fusion
  153.8 13.1 %all_to_all.32 = f32[8,4,640]{2,1,0:T(4,128)S(1)} all-to-all(f32[8,4,640]{2,1,0:T(4,128)S(1)} %broadcast_in_dim.6), channel_id=1, replica_groups=mesh['tile'=64,'dp'=8] {'dp'}, dimensions={0} | all-to-all | bytes 163840 | tf_op jit(solution)/shard_map/all_to_all | solution.py:286
  167.0 0.1 broadcast_in_dim.7
  167.1 20.2 %all_to_all.33 = bf16[64,4,640]{2,1,0:T(4,128)(2,1)S(1)} all-to-all(bf16[64,4,640]{2,1,0:T(4,128)(2,1)S(1)} %broadcast_in_dim.7), channel_id=1, replica_groups=mesh['tile'=64,'dp'=8] {'tile'}, dimensions={0} | all-to-all | bytes 655360 | tf_op jit(solution)/shard_map/all_to_all | solution.py:274
  187.3 1.0 reshape.56
  188.4 0.7 reshape.57
  189.1 0.0 reduce-scatter.2.cloned.1.call-done
  (10 shorter events, 0.2 us)
Async XLA Ops:
  7.2 48.3 %all-gather.2.cloned.1.call-start = ((), (), s32[]{:S(2)}) async-start(), calls=%async_computation.7 | async-start | bytes 2359296 | tf_op jit(solution)/shard_map/all_gather | solution.py:301
  7.9 0.7 copy-start
  8.6 0.7 copy-start.2
  9.3 0.7 copy-start.3
  11.5 25.2 %all-to-all-start = ((f32[64,4,128]{2,1,0:T(4,128)}), f32[64,4,128]{2,1,0:T(4,128)S(1)}, u32[]{:S(2)}, u32[]{:S(2)}) async-start(f32[64,4,128]{2,1,0:T(4,128)} %get-tuple-element.12), calls=%async_computation | async-start | bytes 262144 | tf_op jit(solution)/shard_map/all_to_all | solution.py:274
  36.8 58.0 %copy-start.1 = (s32[1024,1]{0,1:T(1,128)S(1)}, s32[1024,1]{0,1:T(1,128)}, u32[]{:S(2)}) copy-start(s32[1024,1]{0,1:T(1,128)} %param.7) | copy-start | bytes 12292
  36.8 58.0 %copy-start.4 = (f32[3,64]{1,0:T(4,128)S(1)}, f32[3,64]{1,0:T(4,128)}, u32[]{:S(2)}) copy-start(f32[3,64]{1,0:T(4,128)} %targets_ref.1) | copy-start | bytes 2308
  98.2 14.4 %all-to-all-start.2 = ((f32[64,2,128]{2,1,0:T(2,128)}), f32[64,2,128]{2,1,0:T(2,128)S(1)}, u32[]{:S(2)}, u32[]{:S(2)}) async-start(f32[64,2,128]{2,1,0:T(2,128)} %reshape.51), calls=%async_computation.2 | async-start | bytes 131072 | tf_op jit(solution)/shard_map/all_to_all | solution.py:274
  102.7 86.4 %reduce-scatter.2.cloned.1.call-start = ((), (), s32[]{:S(2)}) async-start(), calls=%async_computation.8 | async-start | bytes 4718592 | tf_op jit(solution)/shard_map/reduce_scatter | solution.py:333
  135.1 0.9 copy-start.5
  135.1 1.0 copy-start.6
Sparse Core Ops, SparseCore 0:
  10.1 45.3 all-gather.1
  135.3 51.6 reduce-scatter.1

commit v3 on v2

--- a/solution.py
+++ b/solution.py
@@ -28,18 +28,38 @@
     return lax.broadcasted_iota(jnp.int32, shape, dim)
 
 
-def slot_kernel(tile_ref, corners_ref, offsets_ref, send_ref, rank_ref, *, tiles, capacity):
+def slot_kernel(
+    tile_ref, corners_ref, offsets_ref, tile_column_ref, row_column_ref, send_ref, slot_ref,
+    *, tiles, capacity,
+):
     tile = tile_ref[...]
     samples = tile.shape[1]
     members = row_iota((tiles, samples), 0) == tile
     member_rows = members.astype(f32).astype(bf16)
-    before = (
-        row_iota((samples, samples), 0) < row_iota((samples, samples), 1)
-    ).astype(f32).astype(bf16)
-    earlier = matmul(member_rows, before)
-    rank = jnp.sum(jnp.where(members, earlier, 0.0), axis=0, keepdims=True)
-    rank_ref[...] = rank
-    at_rank = row_iota((capacity, samples), 0) == rank.astype(jnp.int32)
+    order = corners_ref[0:1] * samples + row_iota((1, samples), 1)
+    part = 128
+    rank = jnp.zeros((1, samples), f32)
+    count = jnp.zeros((1, samples), f32)
+    for first in range(0, samples, part):
+        here = slice(first, first + part)
+        same = tile_column_ref[here] == tile
+        order_column = row_column_ref[here] * samples + row_iota((part, 1), 0) + first
+        rank += jnp.sum(jnp.where(same & (order_column < order), 1.0, 0.0), axis=0, keepdims=True)
+        count += jnp.sum(jnp.where(same, 1.0, 0.0), axis=0, keepdims=True)
+    lead = jnp.full((1, samples), -float(samples), f32)
+    for first in range(0, samples, part):
+        here = slice(first, first + part)
+        same = tile_column_ref[here] == tile
+        row_column = row_column_ref[here]
+        order_column = row_column * samples + row_iota((part, 1), 0) + first
+        rank_column = jnp.sum(
+            jnp.where(same & (order < order_column), 1.0, 0.0), axis=1, keepdims=True
+        )
+        ahead = jnp.where(same & (order_column <= order), row_column.astype(f32) - rank_column, -1e4)
+        lead = jnp.maximum(lead, jnp.max(ahead, axis=0, keepdims=True))
+    slot = rank + jnp.minimum(lead, float(capacity) - count)
+    slot_ref[...] = slot
+    at_slot = row_iota((capacity, samples), 0) == slot.astype(jnp.int32)
     along = offsets_ref[0:1]
     across = offsets_ref[1:2]
     fields = [
@@ -52,7 +72,7 @@
     ]
     for pair in range(FIELDS // 2):
         placed = jnp.concatenate(
-            [jnp.where(at_rank, field, 0.0) for field in fields[2 * pair : 2 * pair + 2]], axis=0
+            [jnp.where(at_slot, field, 0.0) for field in fields[2 * pair : 2 * pair + 2]], axis=0
         )
         send_ref[:, pair, :] = matmul(member_rows, placed.astype(bf16), ((1,), (1,)))
     send_ref[:, FIELDS // 2, :] = jnp.zeros((tiles, 2 * capacity), f32)
@@ -83,62 +103,108 @@
     return 0.5 + 0.5 * jnp.tanh(0.5 * x)
 
 
+WINDOWS = (16, 24, 32, 40, GSIDE)
+ALIGN = 4
+
+
+def in_window(least, most, run):
+    begin = jnp.minimum(jnp.maximum(least, 0), GSIDE - 1) // ALIGN * ALIGN
+    need = most + 1 - begin
+    smaller = -GSIDE
+    for size in WINDOWS:
+        fits = need <= size if size < GSIDE else need > smaller
+
+        @pl.when((need > smaller) & fits)
+        def _(size=size):
+            run(jnp.minimum(begin, GSIDE - size), size)
+
+        smaller = size
+
+
+def window_bounds(info, block):
+    slots = info.shape[1]
+    filled = jnp.sum(info[2:6], axis=0) > 0.0
+    row = info[0].astype(jnp.int32)
+    by_block = lambda x: x.reshape(slots // block, block)
+    least = jnp.min(by_block(jnp.where(filled, row, GSIDE - 1)), axis=1)
+    most = jnp.max(by_block(jnp.where(filled, row + 1, 0)), axis=1)
+    number = jnp.arange(slots, dtype=jnp.int32) // (slots // GSIDE)
+    group = jnp.arange(0, GSIDE, block * GSIDE // slots, dtype=jnp.int32)[:, None]
+    touches = filled & (row + 1 >= group) & (row < group + block * GSIDE // slots)
+    first = jnp.min(jnp.where(touches, number, GSIDE - 1), axis=1)
+    last = jnp.max(jnp.where(touches, number, 0), axis=1)
+    return jnp.stack([least, most, first, last])
+
+
+def small(value):
+    return jnp.full((1, 1), value, jnp.int32).astype(f32).astype(bf16)
+
+
 def forward_kernel(
-    info_ref, grid_ref, first_t_ref, second_t_ref, features_ref, decoded_ref, weights_ref, *, rows
+    bounds_ref, info_ref, grid_ref, first_t_ref, second_t_ref,
+    features_ref, decoded_ref, weights_ref, *, rows,
 ):
     row, upper, lower = sample_columns(info_ref[...].astype(bf16))
-    cells = rows * GSIDE
-    total = None
-    for first_row in range(0, GSIDE, rows):
-        here = pl.ds(first_row * GSIDE, cells)
-        for a, piece in weight_rows(row - float(first_row), upper, lower, rows):
-            weights_ref[pl.ds((first_row + a) * GSIDE, GSIDE), :] = piece
-        term = matmul(grid_ref[:, here], weights_ref[here, :])
-        total = term if total is None else total + term
-    features = total.astype(bf16)
-    features_ref[...] = features
-    pre_act = matmul(first_t_ref[...], features)
+
+    def gather(start, size):
+        local = row - small(start)
+        total = None
+        for first_row in range(0, size, rows):
+            here = pl.ds(first_row * GSIDE, rows * GSIDE)
+            for a, piece in weight_rows(local - float(first_row), upper, lower, rows):
+                weights_ref[pl.ds((first_row + a) * GSIDE, GSIDE), :] = piece
+            there = pl.multiple_of((start + first_row) * GSIDE, ALIGN * GSIDE)
+            term = matmul(grid_ref[:, pl.ds(there, rows * GSIDE)], weights_ref[here, :])
+            total = term if total is None else total + term
+        features_ref[...] = total.astype(bf16)
+
+    step = pl.program_id(0)
+    in_window(bounds_ref[0, step], bounds_ref[1, step], gather)
+    pre_act = matmul(first_t_ref[...], features_ref[...])
     hidden = (pre_act * logistic(pre_act)).astype(bf16)
     decoded_ref[...] = matmul(second_t_ref[...], hidden)[0:4]
 
 
-def forward_call(info, grid_table, first_t, second_t, block=1024, rows=8):
+def forward_call(bounds, info, grid_table, first_t, second_t, block, rows=8):
     channels, cells = grid_table.shape
     hid = first_t.shape[0]
     slots = info.shape[1]
-    whole = lambda s: (0, 0)
-    part = lambda s: (0, s)
+    whole = lambda s, bounds: (0, 0)
+    part = lambda s, bounds: (0, s)
     return pl.pallas_call(
         functools.partial(forward_kernel, rows=rows),
-        grid=(slots // block,),
-        in_specs=[
-            pl.BlockSpec((8, block), part),
-            pl.BlockSpec((channels, cells), whole),
-            pl.BlockSpec((hid, channels), whole),
-            pl.BlockSpec((16, hid), whole),
-        ],
-        out_specs=[pl.BlockSpec((channels, block), part), pl.BlockSpec((4, block), part)],
+        grid_spec=pltpu.PrefetchScalarGridSpec(
+            num_scalar_prefetch=1,
+            grid=(slots // block,),
+            in_specs=[
+                pl.BlockSpec((8, block), part),
+                pl.BlockSpec((channels, cells), whole),
+                pl.BlockSpec((hid, channels), whole),
+                pl.BlockSpec((16, hid), whole),
+            ],
+            out_specs=[pl.BlockSpec((channels, block), part), pl.BlockSpec((4, block), part)],
+            scratch_shapes=[pltpu.VMEM((cells, block), bf16)],
+        ),
         out_shape=[
             jax.ShapeDtypeStruct((channels, slots), bf16),
             jax.ShapeDtypeStruct((4, slots), f32),
         ],
-        scratch_shapes=[pltpu.VMEM((cells, block), bf16)],
         compiler_params=pltpu.CompilerParams(vmem_limit_bytes=VMEM_BYTES),
-    )(info, grid_table, first_t, second_t)
-
-
-def shade_kernel(tile_ref, rank_ref, back_ref, targets_ref, send_ref, *, tiles, capacity):
+    )(bounds, info, grid_table, first_t, second_t)
+
+
+def shade_kernel(tile_ref, slot_ref, back_ref, targets_ref, send_ref, *, tiles, capacity):
     tile = tile_ref[...]
     samples = tile.shape[1]
     rays = targets_ref.shape[1]
     members = (row_iota((tiles, samples), 0) == tile).astype(f32)
-    at_rank = row_iota((capacity, samples), 0) == rank_ref[...].astype(jnp.int32)
+    at_slot = row_iota((capacity, samples), 0) == slot_ref[...].astype(jnp.int32)
     decoded = []
     for number in range(4):
         spread = matmul(
             back_ref[:, number * capacity : (number + 1) * capacity], members, ((0,), (0,)), HIGHEST
         )
-        decoded.append(jnp.sum(jnp.where(at_rank, spread, 0.0), axis=0, keepdims=True))
+        decoded.append(jnp.sum(jnp.where(at_slot, spread, 0.0), axis=0, keepdims=True))
     raw = decoded[0]
     ray_of = row_iota((rays, samples), 1) // (MARCH + 1) == row_iota((rays, samples), 0)
     first = row_iota((rays, samples), 1) == row_iota((rays, samples), 0) * (MARCH + 1)
@@ -164,7 +230,7 @@
     )
     grads = [march_all * jax.nn.sigmoid(raw)] + [surface_all[k : k + 1] for k in range(3)]
     for number in range(4):
-        placed = jnp.where(at_rank, grads[number], 0.0)
+        placed = jnp.where(at_slot, grads[number], 0.0)
         send_ref[:, number * capacity : (number + 1) * capacity] = matmul(
             members, placed, along_rays, HIGHEST
         )
@@ -242,32 +308,43 @@
     )(grads, features, first_t, first, second)
 
 
-def spread_kernel(info_ref, grads_ref, out_ref, weights_ref, *, slot_block):
+def spread_kernel(bounds_ref, info_ref, grads_ref, out_ref, weights_ref, *, numbers):
     rows = out_ref.shape[1] // GSIDE
-    start = jnp.full((1, 1), pl.program_id(0) * rows, jnp.int32).astype(f32).astype(bf16)
-    total = None
-    for s in range(0, info_ref.shape[1], slot_block):
-        here = slice(s, s + slot_block)
-        row, upper, lower = sample_columns(info_ref[:, here].astype(bf16))
-        for a, piece in weight_rows(row - start, upper, lower, rows):
-            weights_ref[pl.ds(a * GSIDE, GSIDE), here] = piece
-        term = matmul(grads_ref[:, here], weights_ref[:, here], ((1,), (1,)))
-        total = term if total is None else total + term
-    out_ref[...] = total
-
-
-def spread_call(info, grads, cells, block=1024, slot_block=512):
+    step = pl.program_id(0)
+    lanes = info_ref.shape[1] // GSIDE
+
+    def scatter(start, size):
+        total = None
+        for number in range(0, size, numbers):
+            there = pl.ds(
+                pl.multiple_of((start + number) * lanes, ALIGN * lanes), numbers * lanes
+            )
+            here = slice(number * lanes, (number + numbers) * lanes)
+            row, upper, lower = sample_columns(info_ref[:, there].astype(bf16))
+            for a, piece in weight_rows(row - small(step * rows), upper, lower, rows):
+                weights_ref[pl.ds(a * GSIDE, GSIDE), here] = piece
+            term = matmul(grads_ref[:, there], weights_ref[:, here], ((1,), (1,)))
+            total = term if total is None else total + term
+        out_ref[...] = total
+
+    in_window(bounds_ref[2, step], bounds_ref[3, step], scatter)
+
+
+def spread_call(bounds, info, grads, cells, block, numbers=8):
     channels, slots = grads.shape
-    whole = lambda s: (0, 0)
+    whole = lambda s, bounds: (0, 0)
     return pl.pallas_call(
-        functools.partial(spread_kernel, slot_block=slot_block),
-        grid=(cells // block,),
-        in_specs=[pl.BlockSpec((8, slots), whole), pl.BlockSpec((channels, slots), whole)],
-        out_specs=pl.BlockSpec((channels, block), lambda s: (0, s)),
+        functools.partial(spread_kernel, numbers=numbers),
+        grid_spec=pltpu.PrefetchScalarGridSpec(
+            num_scalar_prefetch=1,
+            grid=(cells // block,),
+            in_specs=[pl.BlockSpec((8, slots), whole), pl.BlockSpec((channels, slots), whole)],
+            out_specs=pl.BlockSpec((channels, block), lambda s, bounds: (0, s)),
+            scratch_shapes=[pltpu.VMEM((block, slots), bf16)],
+        ),
         out_shape=jax.ShapeDtypeStruct((channels, cells), f32),
-        scratch_shapes=[pltpu.VMEM((block, slots), bf16)],
         compiler_params=pltpu.CompilerParams(vmem_limit_bytes=VMEM_BYTES),
-    )(info, grads)
+    )(bounds, info, grads)
 
 
 def over_tile(x):
@@ -300,36 +377,38 @@
     tile_row = tile_ids.reshape(1, samples)
     grid_table = lax.all_gather(grid, "dp", axis=0, tiled=True)
 
-    send_info, rank = pl.pallas_call(
+    send_info, slot = pl.pallas_call(
         functools.partial(slot_kernel, tiles=owners, capacity=capacity),
         out_shape=[
             jax.ShapeDtypeStruct((owners, FIELDS // 2 + 1, 2 * capacity), f32),
             jax.ShapeDtypeStruct((1, samples), f32),
         ],
         compiler_params=pltpu.CompilerParams(vmem_limit_bytes=SMALL_VMEM_BYTES),
-    )(tile_row, corners, offsets)
+    )(tile_row, corners, offsets, tile_ids, corners[0].reshape(samples, 1))
     first_t = w_first.T
     second_8 = jnp.pad(w_second, ((0, 0), (0, 4)))
     second_t = jnp.pad(second_8, ((0, 0), (0, 8))).T
-    info = over_tile(send_info).reshape(owners, 8, capacity).transpose(1, 0, 2)
+    info = over_tile(send_info).reshape(owners, 8, capacity).transpose(1, 2, 0)
     info = info.reshape(8, slot_count)
-
-    features, decoded = forward_call(info, grid_table, first_t, second_t)
-
-    back = over_tile(decoded.reshape(4, owners, capacity).transpose(1, 0, 2).reshape(owners, 2, -1))
+    block = 512
+    bounds = window_bounds(info, block)
+
+    features, decoded = forward_call(bounds, info, grid_table, first_t, second_t, block)
+
+    back = over_tile(decoded.reshape(4, capacity, owners).transpose(2, 0, 1).reshape(owners, 2, -1))
     send_grads = pl.pallas_call(
         functools.partial(shade_kernel, tiles=owners, capacity=capacity),
         out_shape=jax.ShapeDtypeStruct((owners, 4 * capacity), f32),
         compiler_params=pltpu.CompilerParams(vmem_limit_bytes=SMALL_VMEM_BYTES),
-    )(tile_row, rank, back.reshape(owners, 4 * capacity), targets)
+    )(tile_row, slot, back.reshape(owners, 4 * capacity), targets)
     grads = over_tile(send_grads.reshape(owners, 2, -1))
-    grads = grads.reshape(owners, 4, capacity).transpose(1, 0, 2).reshape(4, slot_count)
+    grads = grads.reshape(owners, 4, capacity).transpose(1, 2, 0).reshape(4, slot_count)
 
     second_24 = jnp.concatenate([second_8] * 3, axis=1)
     feature_grad, grad_first, grad_second = backward_call(
         grads, features, first_t, w_first, second_24
     )
-    share = spread_call(info, feature_grad, cells)
+    share = spread_call(bounds, info, feature_grad, cells, block)
     grid_grad = lax.psum_scatter(share, "dp", scatter_dimension=0, tiled=True)
     share, grad_first, grad_second = lax.optimization_barrier((share, grad_first, grad_second))
     grad_first, grad_second = all_sum(grad_first, grad_second)

time: 197 us -> 191 us (0.970)
  Pallas kernels: 39.7 us -> 35 us
  waiting for transfers between devices: 34.7 us -> 31 us
    pallas_call x2, Pallas kernels: 26.1 us -> 19.1 us  [the longest x1 10.8 us: forward_call(): pl.pallas_call(functools.partial(forward_kernel, rows=rows), grid_spec=pl...]
    all_gather x1, waiting for transfers between devices: 17.9 us -> 12.3 us  [body(): grid_table = lax.all_gather(grid, 'dp', axis=0, tiled=True)]
    pallas_call x1, Pallas kernels: 1.48 us -> 3.71 us  [body(): pl.pallas_call(functools.partial(slot_kernel, tiles=owners, capacity=capa...]
    unnamed x17 -> x22, local copies, waits for them, and re-layouts: 4.87 us -> 4.84 us
  transfers between devices with their start and end apart: 4 -> 4, of which waited for: 3 -> 3; matrix products, arithmetic and copies ran while one was open for 4% -> 5% of each run, Pallas kernels for 1% -> 2%
where the time goes in v3:
time: 191 us; the launch traced here: 190 us
  blocking collectives  76 us (40%)
  Pallas kernels  35 us (18%)
  waiting for transfers between devices  31 us (16%)
  starting transfers between devices  19.4 us (10%)
  between operations  14.3 us (7%)
  local copies, waits for them, and re-layouts  12.9 us (7%)
    all_to_all x3, blocking collectives, over_tile(): return lax.all_to_all(x, 'tile', split_axis=0, concat_axis=0, tiled=True)  62.7 us
    all_to_all x2, starting transfers between devices, over_tile(): return lax.all_to_all(x, 'tile', split_axis=0, concat_axis=0, tiled=True)  19.3 us
    all_to_all x2, waiting for transfers between devices, over_tile(): return lax.all_to_all(x, 'tile', split_axis=0, concat_axis=0, tiled=True)  18 us
    all_to_all x1, blocking collectives, all_sum(): lax.all_to_all(copies, 'dp', split_axis=0, concat_axis=0, tiled=True)  13.3 us
    all_gather x1, waiting for transfers between devices, body(): grid_table = lax.all_gather(grid, 'dp', axis=0, tiled=True)  12.3 us
    pallas_call x1, Pallas kernels, forward_call(): pl.pallas_call(functools.partial(forward_kernel, rows=rows), grid_spec=pl...  10.8 us
    pallas_call x1, Pallas kernels, backward_call(): pl.pallas_call(backward_kernel, grid=(slots // block,), in_specs=[pl.Bloc...  9.41 us
    pallas_call x1, Pallas kernels, spread_call(): pl.pallas_call(functools.partial(spread_kernel, numbers=numbers), grid_sp...  8.29 us
  transfers between devices with their start and end apart: 4, of which 3 were waited for; matrix products, arithmetic and copies ran while one was open for 5% of the time, Pallas kernels for 2%

profile of v3, /device:TPU:1, one launch (start us, length us, event | category | flops | bytes accessed | tf_op | source)
XLA Modules:
  0.0 190.2 jit_solution(5681024317652033362)
XLA Ops:
  7.2 0.0 copy-start.5
  7.2 0.0 copy-start.8
  7.2 0.0 all-gather.2.cloned.1.call-start
  7.2 0.7 all-gather.2.cloned.1.call-update
  7.9 0.7 slice_bitcast_fusion.1
  8.6 0.2 copy.48.row_column_ref
  8.9 0.9 copy.47.tile_column_ref
  9.8 0.0 copy-start
  9.8 0.7 copy-done
  10.5 0.0 copy-start.2
  10.5 0.7 copy-done.2
  11.2 0.0 copy-start.3
  11.2 0.7 copy-done.3
  11.9 3.7 %shard_map.94 = (f32[64,4,128]{2,1,0:T(4,128)}, f32[1,1024]{1,0:T(1,128)S(1)}) custom-call(s32[1,1024]{1,0:T(1,128)S(1)} %bitcast.38, s32[2,1024]{1,0:T(2,128)S(1)} %copy-done.2, f32[2,1024]{1,0:T(2,128)S(1)} %copy-done.3, s32[1024,1]{1,0:T(8,128)S(1)} %copy.47.tile_column_ref, s32[1024,1]{1,0:T(8,128)S(1)} %copy.48.row_column_ref), custom_call_target="tpu_custom_call" | custom-call | tf_op jit(solution)/shard_map/pallas_call | solution.py:380
  15.6 14.8 %all-to-all-start = ((f32[64,4,128]{2,1,0:T(4,128)}), f32[64,4,128]{2,1,0:T(4,128)S(1)}, u32[]{:S(2)}, u32[]{:S(2)}) async-start(f32[64,4,128]{2,1,0:T(4,128)} %get-tuple-element.12), calls=%async_computation | async-start | bytes 262144 | tf_op jit(solution)/shard_map/all_to_all | solution.py:351
  30.4 0.0 copy-done.5
  30.4 0.8 copy.50
  31.3 0.0 copy-done.8
  31.3 0.6 pad_bitcast_fusion.second_t_ref
  31.9 8.9 %all-to-all-done = f32[64,4,128]{2,1,0:T(4,128)S(1)} async-done(((f32[64,4,128]{2,1,0:T(4,128)}), f32[64,4,128]{2,1,0:T(4,128)S(1)}, u32[]{:S(2)}, u32[]{:S(2)}) %all-to-all-start) | async-done | bytes 131104 | tf_op jit(solution)/shard_map/all_to_all | solution.py:351
  40.8 0.1 copy.57
  40.9 0.0 copy-start.1
  40.9 0.0 copy-start.4
  40.9 0.8 reshape.90.info_ref
  41.7 0.1 convert_element_type.40
  41.8 0.1 fusion.2
  41.9 0.1 reduce_min.26
  42.0 0.1 reduce_max.26
  42.1 0.1 gt.19
  42.2 0.1 reduce_min.27
  42.3 0.1 reduce_max.27
  42.4 0.3 select_reduce_fusion.1
  42.7 0.6 pad_add_fusion.bounds_ref
  43.3 12.3 %all-gather.2.cloned.1.call-done.grid_ref = bf16[256,4096]{1,0:T(8,128)(2,1)} async-done(((bf16[32,4096]{1,0:T(8,128)(2,1)}), bf16[256,4096]{1,0:T(8,128)(2,1)}) %all-gather.2.cloned.1.call-update) | async-done | bytes 2097168 | tf_op jit(solution)/shard_map/all_gather | solution.py:378
  55.6 10.8 %shard_map.95 = (bf16[256,4096]{1,0:T(8,128)(2,1)}, f32[4,4096]{1,0:T(4,128)}) custom-call(s32[4,8]{1,0:T(4,128)} %pad_add_fusion.bounds_ref, f32[8,4096]{1,0:T(8,128)} %reshape.90.info_ref, bf16[256,4096]{1,0:T(8,128)(2,1)} %all-gather.2.cloned.1.call-done.grid_ref, bf16[512,256]{1,0:T(8,128)(2,1)} %bitcast.40, bf16[16,512]{1,0:T(8,128)(2,1)} %pad_bitcast_fusion.second_t_ref), custom_call_target="tpu_custom_call" | custom-call | tf_op jit(solution)/shard_map/pallas_call | solution.py:174
  66.4 1.0 reshape.91
  67.3 0.1 copy.58
  67.4 24.8 %all_to_all.30 = f32[64,2,128]{2,1,0:T(2,128)S(1)} all-to-all(f32[64,2,128]{2,1,0:T(2,128)S(1)} %copy.58), channel_id=1, replica_groups=mesh['tile'=64,'dp'=8] {'tile'}, dimensions={0} | all-to-all | bytes 131072 | tf_op jit(solution)/shard_map/all_to_all | solution.py:351
  92.3 0.0 copy-done.1
  92.3 0.0 copy-done.4
  92.3 2.8 %shard_map.96 = f32[64,256]{1,0:T(8,128)S(1)} custom-call(s32[1,1024]{1,0:T(1,128)S(1)} %bitcast.39, f32[1,1024]{1,0:T(1,128)S(1)} %get-tuple-element.13.slot_ref, f32[64,256]{1,0:T(8,128)S(1)} %bitcast.37, f32[3,64]{1,0:T(4,128)S(1)} %copy-done.4), custom_call_target="tpu_custom_call" | custom-call | tf_op jit(solution)/shard_map/pallas_call | solution.py:399
  95.1 0.7 reshape.94
  95.8 4.4 %all-to-all-start.2 = ((f32[64,2,128]{2,1,0:T(2,128)}), f32[64,2,128]{2,1,0:T(2,128)S(1)}, u32[]{:S(2)}, u32[]{:S(2)}) async-start(f32[64,2,128]{2,1,0:T(2,128)} %reshape.94), calls=%async_computation.2 | async-start | bytes 131072 | tf_op jit(solution)/shard_map/all_to_all | solution.py:351
  100.2 0.0 reduce-scatter.2.cloned.1.call-start
  100.3 0.8 copy.53.second_ref
  101.0 9.1 %all-to-all-done.2 = f32[64,2,128]{2,1,0:T(2,128)S(1)} async-done(((f32[64,2,128]{2,1,0:T(2,128)}), f32[64,2,128]{2,1,0:T(2,128)S(1)}, u32[]{:S(2)}, u32[]{:S(2)}) %all-to-all-start.2) | async-done | bytes 65568 | tf_op jit(solution)/shard_map/all_to_all | solution.py:351
  110.1 0.1 copy.52
  110.2 0.7 reshape.96.grads_ref
  110.9 9.4 %shard_map.97 = (bf16[256,4096]{1,0:T(8,128)(2,1)}, bf16[256,512]{1,0:T(8,128)(2,1)}, f32[4,512]{1,0:T(4,128)}) custom-call(f32[4,4096]{1,0:T(4,128)} %reshape.96.grads_ref, bf16[256,4096]{1,0:T(8,128)(2,1)} %get-tuple-element.15.features_ref, bf16[512,256]{1,0:T(8,128)(2,1)} %bitcast.41, bf16[256,512]{1,0:T(8,128)(2,1)} %first_ref.1, ...), custom_call_target="tpu_custom_call" | custom-call | tf_op jit(solution)/shard_map/pallas_call | solution.py:286
  120.3 8.3 %shard_map.98 = f32[256,4096]{1,0:T(8,128)} custom-call(s32[4,8]{1,0:T(4,128)} %pad_add_fusion.bounds_ref, f32[8,4096]{1,0:T(8,128)} %reshape.90.info_ref, bf16[256,4096]{1,0:T(8,128)(2,1)} %get-tuple-element.16.grads_ref), custom_call_target="tpu_custom_call" | custom-call | tf_op jit(solution)/shard_map/pallas_call | solution.py:336
  128.6 0.0 reduce-scatter.2.cloned.1.call-update
  128.7 0.9 copy-done.6
  129.6 0.1 reshape.97
  129.7 0.0 copy-done.7
  129.7 0.1 reshape.98
  129.8 0.1 copy.60
  129.9 0.2 fusion.1
  130.0 17.7 %all_to_all.31 = bf16[64,4,640]{2,1,0:T(4,128)(2,1)S(1)} all-to-all(bf16[64,4,640]{2,1,0:T(4,128)(2,1)S(1)} %fusion.1), channel_id=1, replica_groups=mesh['tile'=64,'dp'=8] {'tile'}, dimensions={0} | all-to-all | bytes 655360 | tf_op jit(solution)/shard_map/all_to_all | solution.py:351
  147.7 0.2 convert_reduce_fusion
  147.9 13.3 %all_to_all.32 = f32[8,4,640]{2,1,0:T(4,128)S(1)} all-to-all(f32[8,4,640]{2,1,0:T(4,128)S(1)} %broadcast_in_dim.39), channel_id=1, replica_groups=mesh['tile'=64,'dp'=8] {'dp'}, dimensions={0} | all-to-all | bytes 163840 | tf_op jit(solution)/shard_map/all_to_all | solution.py:363
  161.2 0.1 broadcast_in_dim.40
  161.3 20.2 %all_to_all.33 = bf16[64,4,640]{2,1,0:T(4,128)(2,1)S(1)} all-to-all(bf16[64,4,640]{2,1,0:T(4,128)(2,1)S(1)} %broadcast_in_dim.40), channel_id=1, replica_groups=mesh['tile'=64,'dp'=8] {'tile'}, dimensions={0} | all-to-all | bytes 655360 | tf_op jit(solution)/shard_map/all_to_all | solution.py:351
  181.5 1.0 reshape.99
  182.6 0.7 reshape.100
  (17 shorter events, 0.2 us)
Async XLA Ops:
  7.2 23.2 %copy-start.5 = (bf16[256,512]{1,0:T(8,128)(2,1)S(1)}, bf16[256,512]{1,0:T(8,128)(2,1)}, u32[]{:S(2)}) copy-start(bf16[256,512]{1,0:T(8,128)(2,1)} %first_ref.1) | copy-start | bytes 786436
  7.2 24.1 %copy-start.8 = (bf16[512,4]{0,1:T(4,128)(2,1)S(1)}, bf16[512,4]{0,1:T(4,128)(2,1)}, u32[]{:S(2)}) copy-start(bf16[512,4]{0,1:T(4,128)(2,1)} %param.13) | copy-start | bytes 12292
  7.2 48.4 %all-gather.2.cloned.1.call-start = ((), (), s32[]{:S(2)}) async-start(), calls=%async_computation.7 | async-start | bytes 2359296 | tf_op jit(solution)/shard_map/all_gather | solution.py:378
  9.8 0.7 copy-start
  10.5 0.7 copy-start.2
  11.2 0.7 copy-start.3
  15.6 25.2 %all-to-all-start = ((f32[64,4,128]{2,1,0:T(4,128)}), f32[64,4,128]{2,1,0:T(4,128)S(1)}, u32[]{:S(2)}, u32[]{:S(2)}) async-start(f32[64,4,128]{2,1,0:T(4,128)} %get-tuple-element.12), calls=%async_computation | async-start | bytes 262144 | tf_op jit(solution)/shard_map/all_to_all | solution.py:351
  40.9 51.4 %copy-start.1 = (s32[1024,1]{0,1:T(1,128)S(1)}, s32[1024,1]{0,1:T(1,128)}, u32[]{:S(2)}) copy-start(s32[1024,1]{0,1:T(1,128)} %param.7) | copy-start | bytes 12292
  40.9 51.4 %copy-start.4 = (f32[3,64]{1,0:T(4,128)S(1)}, f32[3,64]{1,0:T(4,128)}, u32[]{:S(2)}) copy-start(f32[3,64]{1,0:T(4,128)} %targets_ref.1) | copy-start | bytes 2308
  95.8 14.4 %all-to-all-start.2 = ((f32[64,2,128]{2,1,0:T(2,128)}), f32[64,2,128]{2,1,0:T(2,128)S(1)}, u32[]{:S(2)}, u32[]{:S(2)}) async-start(f32[64,2,128]{2,1,0:T(2,128)} %reshape.94), calls=%async_computation.2 | async-start | bytes 131072 | tf_op jit(solution)/shard_map/all_to_all | solution.py:351
  100.2 83.1 %reduce-scatter.2.cloned.1.call-start = ((), (), s32[]{:S(2)}) async-start(), calls=%async_computation.8 | async-start | bytes 4718592 | tf_op jit(solution)/shard_map/reduce_scatter | solution.py:412
  128.6 0.9 copy-start.6
  128.6 1.0 copy-start.7
Sparse Core Ops, SparseCore 0:
  10.1 45.4 all-gather.1
  128.8 52.3 reduce-scatter.1

commit v4 on v3

--- a/solution.py
+++ b/solution.py
@@ -16,7 +16,7 @@
 f32 = jnp.float32
 HIGHEST = lax.Precision.HIGHEST
 FIELDS = 6
-VMEM_BYTES = 56 << 20
+VMEM_BYTES = 40 << 20
 SMALL_VMEM_BYTES = 12 << 20
 
 
@@ -390,7 +390,7 @@
     second_t = jnp.pad(second_8, ((0, 0), (0, 8))).T
     info = over_tile(send_info).reshape(owners, 8, capacity).transpose(1, 2, 0)
     info = info.reshape(8, slot_count)
-    block = 512
+    block = 1024
     bounds = window_bounds(info, block)
 
     features, decoded = forward_call(bounds, info, grid_table, first_t, second_t, block)

time: 191 us -> 184 us (0.963)
  Pallas kernels: 35 us -> 27.1 us
  waiting for transfers between devices: 31 us -> 33.9 us
    pallas_call x1, Pallas kernels: 8.29 us -> 5.14 us  [spread_call(): pl.pallas_call(functools.partial(spread_kernel, numbers=numbers), grid_sp...]
    pallas_call x1, Pallas kernels: 10.8 us -> 7.76 us  [forward_call(): pl.pallas_call(functools.partial(forward_kernel, rows=rows), grid_spec=pl...]
  transfers between devices with their start and end apart: 4 -> 4, of which waited for: 3 -> 3; matrix products, arithmetic and copies ran while one was open for 5% -> 3% of each run, Pallas kernels for 2% -> 2%
where the time goes in v4:
time: 184 us; the launch traced here: 183 us
  blocking collectives  75.5 us (41%)
  waiting for transfers between devices  33.9 us (18%)
  Pallas kernels  27.1 us (15%)
  starting transfers between devices  19.6 us (11%)
  between operations  14.3 us (8%)
  local copies, waits for them, and re-layouts  11.5 us (6%)
    all_to_all x3, blocking collectives, over_tile(): return lax.all_to_all(x, 'tile', split_axis=0, concat_axis=0, tiled=True)  63.1 us
    all_to_all x2, waiting for transfers between devices, over_tile(): return lax.all_to_all(x, 'tile', split_axis=0, concat_axis=0, tiled=True)  19.7 us
    all_to_all x2, starting transfers between devices, over_tile(): return lax.all_to_all(x, 'tile', split_axis=0, concat_axis=0, tiled=True)  19.3 us
    all_gather x1, waiting for transfers between devices, body(): grid_table = lax.all_gather(grid, 'dp', axis=0, tiled=True)  13.5 us
    all_to_all x1, blocking collectives, all_sum(): lax.all_to_all(copies, 'dp', split_axis=0, concat_axis=0, tiled=True)  12.3 us
    pallas_call x1, Pallas kernels, forward_call(): pl.pallas_call(functools.partial(forward_kernel, rows=rows), grid_spec=pl...  7.76 us
    pallas_call x1, Pallas kernels, backward_call(): pl.pallas_call(backward_kernel, grid=(slots // block,), in_specs=[pl.Bloc...  7.73 us
    unnamed x22, local copies, waits for them, and re-layouts  6.71 us
  transfers between devices with their start and end apart: 4, of which 3 were waited for; matrix products, arithmetic and copies ran while one was open for 3% of the time, Pallas kernels for 2%

profile of v4, /device:TPU:1, one launch (start us, length us, event | category | flops | bytes accessed | tf_op | source)
XLA Modules:
  0.0 182.9 jit_solution(14137694869738425789)
XLA Ops:
  7.2 0.0 copy-start.2
  7.2 0.0 copy-start.8
  7.2 0.0 all-gather.2.cloned.1.call-start
  7.2 0.7 all-gather.2.cloned.1.call-update
  7.9 0.7 slice_bitcast_fusion.1
  8.6 0.2 copy.48.row_column_ref
  8.9 0.9 copy.47.tile_column_ref
  9.8 0.0 copy-start.3
  9.8 0.7 copy-done.3
  10.5 0.0 copy-start.5
  10.5 0.7 copy-done.5
  11.2 0.0 copy-start.6
  11.2 0.7 copy-done.6
  11.9 3.7 %shard_map.94 = (f32[64,4,128]{2,1,0:T(4,128)}, f32[1,1024]{1,0:T(1,128)S(1)}) custom-call(s32[1,1024]{1,0:T(1,128)S(1)} %bitcast.40, s32[2,1024]{1,0:T(2,128)S(1)} %copy-done.5, f32[2,1024]{1,0:T(2,128)S(1)} %copy-done.6, s32[1024,1]{1,0:T(8,128)S(1)} %copy.47.tile_column_ref, s32[1024,1]{1,0:T(8,128)S(1)} %copy.48.row_column_ref), custom_call_target="tpu_custom_call" | custom-call | tf_op jit(solution)/shard_map/pallas_call | solution.py:380
  15.6 14.8 %all-to-all-start = ((f32[64,4,128]{2,1,0:T(4,128)}), f32[64,4,128]{2,1,0:T(4,128)S(1)}, u32[]{:S(2)}, u32[]{:S(2)}) async-start(f32[64,4,128]{2,1,0:T(4,128)} %get-tuple-element.12), calls=%async_computation | async-start | bytes 262144 | tf_op jit(solution)/shard_map/all_to_all | solution.py:351
  30.4 0.0 copy-done.2
  30.4 0.1 copy.50
  30.6 0.0 copy-done.8
  30.6 10.2 %all-to-all-done = f32[64,4,128]{2,1,0:T(4,128)S(1)} async-done(((f32[64,4,128]{2,1,0:T(4,128)}), f32[64,4,128]{2,1,0:T(4,128)S(1)}, u32[]{:S(2)}, u32[]{:S(2)}) %all-to-all-start) | async-done | bytes 131104 | tf_op jit(solution)/shard_map/all_to_all | solution.py:351
  40.8 0.1 copy.57
  40.9 0.0 copy-start.4
  40.9 0.0 copy-start.7
  40.9 0.1 reshape.90.info_ref
  41.1 0.1 convert_element_type.40
  41.2 0.1 fusion.2
  41.3 0.1 reduce_min.26
  41.4 0.1 reduce_max.26
  41.4 0.1 gt.19
  41.5 0.1 reduce_min.27
  41.6 0.1 reduce_max.27
  41.8 0.3 select_reduce_fusion.1
  42.1 13.5 %all-gather.2.cloned.1.call-done.grid_ref = bf16[256,4096]{1,0:T(8,128)(2,1)} async-done(((bf16[32,4096]{1,0:T(8,128)(2,1)}), bf16[256,4096]{1,0:T(8,128)(2,1)}) %all-gather.2.cloned.1.call-update) | async-done | bytes 2097168 | tf_op jit(solution)/shard_map/all_gather | solution.py:378
  55.6 0.0 copy-start.1
  55.6 1.6 copy-done.1
  57.2 7.8 %shard_map.95 = (bf16[256,4096]{1,0:T(8,128)(2,1)S(1)}, f32[4,4096]{1,0:T(4,128)S(1)}) custom-call(s32[4,4]{1,0:T(4,128)S(1)} %pad_add_fusion.bounds_ref, f32[8,4096]{1,0:T(8,128)S(1)} %reshape.90.info_ref, bf16[256,4096]{1,0:T(8,128)(2,1)S(1)} %copy-done.1, bf16[512,256]{1,0:T(8,128)(2,1)S(1)} %bitcast.37, bf16[16,512]{1,0:T(8,128)(2,1)S(1)} %pad_bitcast_fusion.second_t_ref), custom_call_target="tpu_custom_call" | custom-call | tf_op jit(solution)/shard_map/pallas_call | solution.py:174
  64.9 0.1 reshape.91
  65.1 0.1 copy.58
  65.2 24.7 %all_to_all.30 = f32[64,2,128]{2,1,0:T(2,128)S(1)} all-to-all(f32[64,2,128]{2,1,0:T(2,128)S(1)} %copy.58), channel_id=1, replica_groups=mesh['tile'=64,'dp'=8] {'tile'}, dimensions={0} | all-to-all | bytes 131072 | tf_op jit(solution)/shard_map/all_to_all | solution.py:351
  89.9 0.0 copy-done.4
  89.9 0.0 copy-done.7
  89.9 2.8 %shard_map.96 = f32[64,256]{1,0:T(8,128)S(1)} custom-call(s32[1,1024]{1,0:T(1,128)S(1)} %bitcast.41, f32[1,1024]{1,0:T(1,128)S(1)} %get-tuple-element.13.slot_ref, f32[64,256]{1,0:T(8,128)S(1)} %bitcast.39, f32[3,64]{1,0:T(4,128)S(1)} %copy-done.7), custom_call_target="tpu_custom_call" | custom-call | tf_op jit(solution)/shard_map/pallas_call | solution.py:399
  92.7 0.7 reshape.94
  93.3 4.4 %all-to-all-start.2 = ((f32[64,2,128]{2,1,0:T(2,128)}), f32[64,2,128]{2,1,0:T(2,128)S(1)}, u32[]{:S(2)}, u32[]{:S(2)}) async-start(f32[64,2,128]{2,1,0:T(2,128)} %reshape.94), calls=%async_computation.2 | async-start | bytes 131072 | tf_op jit(solution)/shard_map/all_to_all | solution.py:351
  97.8 0.3 reduce-scatter.2.cloned.1.call-start
  98.1 0.1 copy.53.second_ref
  98.2 9.5 %all-to-all-done.2 = f32[64,2,128]{2,1,0:T(2,128)S(1)} async-done(((f32[64,2,128]{2,1,0:T(2,128)}), f32[64,2,128]{2,1,0:T(2,128)S(1)}, u32[]{:S(2)}, u32[]{:S(2)}) %all-to-all-start.2) | async-done | bytes 65568 | tf_op jit(solution)/shard_map/all_to_all | solution.py:351
  107.7 0.1 copy.52
  107.8 0.1 reshape.96.grads_ref
  107.9 7.7 %shard_map.97 = (bf16[256,4096]{1,0:T(8,128)(2,1)S(1)}, bf16[256,512]{1,0:T(8,128)(2,1)S(1)}, f32[4,512]{1,0:T(4,128)S(1)}) custom-call(f32[4,4096]{1,0:T(4,128)S(1)} %reshape.96.grads_ref, bf16[256,4096]{1,0:T(8,128)(2,1)S(1)} %get-tuple-element.15.features_ref, bf16[512,256]{1,0:T(8,128)(2,1)S(1)} %bitcast.38, bf16[256,512]{1,0:T(8,128)(2,1)S(1)} %copy-done.2, ...), custom_call_target="tpu_custom_call" | custom-call | tf_op jit(solution)/shard_map/pallas_call | solution.py:286
  115.7 5.1 %shard_map.98 = f32[256,4096]{1,0:T(8,128)S(1)} custom-call(s32[4,4]{1,0:T(4,128)S(1)} %pad_add_fusion.bounds_ref, f32[8,4096]{1,0:T(8,128)S(1)} %reshape.90.info_ref, bf16[256,4096]{1,0:T(8,128)(2,1)S(1)} %get-tuple-element.16.grads_ref), custom_call_target="tpu_custom_call" | custom-call | tf_op jit(solution)/shard_map/pallas_call | solution.py:336
  120.8 0.0 copy-start
  120.8 1.9 %copy-done = f32[256,4096]{1,0:T(8,128)} copy-done((f32[256,4096]{1,0:T(8,128)}, f32[256,4096]{1,0:T(8,128)S(1)}, u32[]{:S(2)}) %copy-start) | copy-done | bytes 4194328
  122.7 0.0 reduce-scatter.2.cloned.1.call-update
  122.7 0.1 reshape.97
  122.8 0.1 reshape.98
  123.0 0.1 copy.60
  123.0 0.2 fusion.1
  123.2 18.2 %all_to_all.31 = bf16[64,4,640]{2,1,0:T(4,128)(2,1)S(1)} all-to-all(bf16[64,4,640]{2,1,0:T(4,128)(2,1)S(1)} %fusion.1), channel_id=1, replica_groups=mesh['tile'=64,'dp'=8] {'tile'}, dimensions={0} | all-to-all | bytes 655360 | tf_op jit(solution)/shard_map/all_to_all | solution.py:351
  141.4 0.2 convert_reduce_fusion
  141.6 12.3 %all_to_all.32 = f32[8,4,640]{2,1,0:T(4,128)S(1)} all-to-all(f32[8,4,640]{2,1,0:T(4,128)S(1)} %broadcast_in_dim.39), channel_id=1, replica_groups=mesh['tile'=64,'dp'=8] {'dp'}, dimensions={0} | all-to-all | bytes 163840 | tf_op jit(solution)/shard_map/all_to_all | solution.py:363
  153.9 0.1 broadcast_in_dim.40
  154.0 20.2 %all_to_all.33 = bf16[64,4,640]{2,1,0:T(4,128)(2,1)S(1)} all-to-all(bf16[64,4,640]{2,1,0:T(4,128)(2,1)S(1)} %broadcast_in_dim.40), channel_id=1, replica_groups=mesh['tile'=64,'dp'=8] {'tile'}, dimensions={0} | all-to-all | bytes 655360 | tf_op jit(solution)/shard_map/all_to_all | solution.py:351
  174.3 1.0 reshape.99
  175.4 0.7 reshape.100
  (17 shorter events, 0.2 us)
Async XLA Ops:
  7.2 23.3 %copy-start.2 = (bf16[256,512]{1,0:T(8,128)(2,1)S(1)}, bf16[256,512]{1,0:T(8,128)(2,1)}, u32[]{:S(2)}) copy-start(bf16[256,512]{1,0:T(8,128)(2,1)} %first_ref.1) | copy-start | bytes 786436
  7.2 23.4 %copy-start.8 = (bf16[512,4]{0,1:T(4,128)(2,1)S(1)}, bf16[512,4]{0,1:T(4,128)(2,1)}, u32[]{:S(2)}) copy-start(bf16[512,4]{0,1:T(4,128)(2,1)} %param.13) | copy-start | bytes 12292
  7.2 48.4 %all-gather.2.cloned.1.call-start = ((), (), s32[]{:S(2)}) async-start(), calls=%async_computation.7 | async-start | bytes 2359296 | tf_op jit(solution)/shard_map/all_gather | solution.py:378
  9.8 0.7 copy-start.3
  10.5 0.7 copy-start.5
  11.2 0.7 copy-start.6
  15.6 25.2 %all-to-all-start = ((f32[64,4,128]{2,1,0:T(4,128)}), f32[64,4,128]{2,1,0:T(4,128)S(1)}, u32[]{:S(2)}, u32[]{:S(2)}) async-start(f32[64,4,128]{2,1,0:T(4,128)} %get-tuple-element.12), calls=%async_computation | async-start | bytes 262144 | tf_op jit(solution)/shard_map/all_to_all | solution.py:351
  40.9 49.0 %copy-start.4 = (s32[1024,1]{0,1:T(1,128)S(1)}, s32[1024,1]{0,1:T(1,128)}, u32[]{:S(2)}) copy-start(s32[1024,1]{0,1:T(1,128)} %param.7) | copy-start | bytes 12292
  40.9 49.0 %copy-start.7 = (f32[3,64]{1,0:T(4,128)S(1)}, f32[3,64]{1,0:T(4,128)}, u32[]{:S(2)}) copy-start(f32[3,64]{1,0:T(4,128)} %targets_ref.1) | copy-start | bytes 2308
  55.6 1.6 copy-start.1
  93.3 14.4 %all-to-all-start.2 = ((f32[64,2,128]{2,1,0:T(2,128)}), f32[64,2,128]{2,1,0:T(2,128)S(1)}, u32[]{:S(2)}, u32[]{:S(2)}) async-start(f32[64,2,128]{2,1,0:T(2,128)} %reshape.94), calls=%async_computation.2 | async-start | bytes 131072 | tf_op jit(solution)/shard_map/all_to_all | solution.py:351
  97.8 78.3 %reduce-scatter.2.cloned.1.call-start = ((), (), s32[]{:S(2)}) async-start(), calls=%async_computation.8 | async-start | bytes 4718592 | tf_op jit(solution)/shard_map/reduce_scatter | solution.py:412
  120.8 1.9 %copy-start = (f32[256,4096]{1,0:T(8,128)}, f32[256,4096]{1,0:T(8,128)S(1)}, u32[]{:S(2)}) copy-start(f32[256,4096]{1,0:T(8,128)S(1)} %shard_map.98) | copy-start | bytes 12582916
Sparse Core Ops, SparseCore 0:
  10.1 45.4 all-gather.1
  122.9 51.9 reduce-scatter.1

commit v5 on v4

--- a/solution.py
+++ b/solution.py
@@ -193,18 +193,26 @@
     )(bounds, info, grid_table, first_t, second_t)
 
 
+def three_pieces(values):
+    high = values.astype(bf16)
+    rest = values - high.astype(f32)
+    mid = rest.astype(bf16)
+    return [high, mid, (rest - mid.astype(f32)).astype(bf16)]
+
+
 def shade_kernel(tile_ref, slot_ref, back_ref, targets_ref, send_ref, *, tiles, capacity):
     tile = tile_ref[...]
     samples = tile.shape[1]
     rays = targets_ref.shape[1]
-    members = (row_iota((tiles, samples), 0) == tile).astype(f32)
+    members = (row_iota((tiles, samples), 0) == tile).astype(f32).astype(bf16)
     at_slot = row_iota((capacity, samples), 0) == slot_ref[...].astype(jnp.int32)
+    spread = matmul(jnp.concatenate(three_pieces(back_ref[...].T), axis=0), members)
+    width = 4 * capacity
+    spread = spread[0:width] + spread[width : 2 * width] + spread[2 * width :]
     decoded = []
     for number in range(4):
-        spread = matmul(
-            back_ref[:, number * capacity : (number + 1) * capacity], members, ((0,), (0,)), HIGHEST
-        )
-        decoded.append(jnp.sum(jnp.where(at_slot, spread, 0.0), axis=0, keepdims=True))
+        own = jnp.where(at_slot, spread[number * capacity : (number + 1) * capacity], 0.0)
+        decoded.append(jnp.sum(own, axis=0, keepdims=True))
     raw = decoded[0]
     ray_of = row_iota((rays, samples), 1) // (MARCH + 1) == row_iota((rays, samples), 0)
     first = row_iota((rays, samples), 1) == row_iota((rays, samples), 0) * (MARCH + 1)
@@ -229,11 +237,12 @@
         precision=HIGHEST,
     )
     grads = [march_all * jax.nn.sigmoid(raw)] + [surface_all[k : k + 1] for k in range(3)]
-    for number in range(4):
-        placed = jnp.where(at_slot, grads[number], 0.0)
-        send_ref[:, number * capacity : (number + 1) * capacity] = matmul(
-            members, placed, along_rays, HIGHEST
+    for pair in range(2):
+        placed = jnp.concatenate(
+            [jnp.where(at_slot, grad, 0.0) for grad in grads[2 * pair : 2 * pair + 2]], axis=0
         )
+        sums = [matmul(members, piece, along_rays) for piece in three_pieces(placed)]
+        send_ref[:, pair, :] = sums[0] + sums[1] + sums[2]
 
 
 def exact_pieces(grads):
@@ -264,10 +273,11 @@
     features = features_ref[...]
     pre_act = matmul(first_t_ref[...], features)
     gate = logistic(pre_act)
-    hidden = (pre_act * gate).astype(bf16)
+    active = pre_act * gate
+    hidden = active.astype(bf16)
     pieces = exact_pieces(grads_ref[...])
     hidden_grad = matmul(second_ref[...], pieces)
-    pre_grad = (hidden_grad * gate * (1.0 + pre_act * (1.0 - gate))).astype(bf16)
+    pre_grad = (hidden_grad * (gate + active * (1.0 - gate))).astype(bf16)
     feature_grad_ref[...] = matmul(first_ref[...], pre_grad).astype(bf16)
     first_sum[...] += matmul(features, pre_grad, ((1,), (1,)))
     second_sum[...] += matmul(pieces, hidden, ((1,), (1,)))
@@ -342,7 +352,7 @@
             out_specs=pl.BlockSpec((channels, block), lambda s, bounds: (0, s)),
             scratch_shapes=[pltpu.VMEM((block, slots), bf16)],
         ),
-        out_shape=jax.ShapeDtypeStruct((channels, cells), f32),
+        out_shape=pltpu.HBM((channels, cells), f32),
         compiler_params=pltpu.CompilerParams(vmem_limit_bytes=VMEM_BYTES),
     )(bounds, info, grads)
 
@@ -398,10 +408,10 @@
     back = over_tile(decoded.reshape(4, capacity, owners).transpose(2, 0, 1).reshape(owners, 2, -1))
     send_grads = pl.pallas_call(
         functools.partial(shade_kernel, tiles=owners, capacity=capacity),
-        out_shape=jax.ShapeDtypeStruct((owners, 4 * capacity), f32),
+        out_shape=jax.ShapeDtypeStruct((owners, 2, 2 * capacity), f32),
         compiler_params=pltpu.CompilerParams(vmem_limit_bytes=SMALL_VMEM_BYTES),
     )(tile_row, slot, back.reshape(owners, 4 * capacity), targets)
-    grads = over_tile(send_grads.reshape(owners, 2, -1))
+    grads = over_tile(send_grads)
     grads = grads.reshape(owners, 4, capacity).transpose(1, 2, 0).reshape(4, slot_count)
 
     second_24 = jnp.concatenate([second_8] * 3, axis=1)

time: 184 us -> 182 us (0.989)
  local copies, waits for them, and re-layouts: 11.5 us -> 8.89 us
    unnamed x22 -> x20, local copies, waits for them, and re-layouts: 6.71 us -> 4.79 us
where the time goes in v5:
time: 182 us
  blocking collectives  76 us (42%)
  waiting for transfers between devices  33.9 us (19%)
  Pallas kernels  27.8 us (15%)
  starting transfers between devices  19.6 us (11%)
  between operations  14.3 us (8%)
  local copies, waits for them, and re-layouts  8.89 us (5%)
    all_to_all x3, blocking collectives, over_tile(): return lax.all_to_all(x, 'tile', split_axis=0, concat_axis=0, tiled=True)  62.7 us
    all_to_all x2, waiting for transfers between devices, over_tile(): return lax.all_to_all(x, 'tile', split_axis=0, concat_axis=0, tiled=True)  19.7 us
    all_to_all x2, starting transfers between devices, over_tile(): return lax.all_to_all(x, 'tile', split_axis=0, concat_axis=0, tiled=True)  19.3 us
    all_gather x1, waiting for transfers between devices, body(): grid_table = lax.all_gather(grid, 'dp', axis=0, tiled=True)  13.5 us
    all_to_all x1, blocking collectives, all_sum(): lax.all_to_all(copies, 'dp', split_axis=0, concat_axis=0, tiled=True)  13.3 us
    pallas_call x1, Pallas kernels, backward_call(): pl.pallas_call(backward_kernel, grid=(slots // block,), in_specs=[pl.Bloc...  8.17 us
    pallas_call x1, Pallas kernels, forward_call(): pl.pallas_call(functools.partial(forward_kernel, rows=rows), grid_spec=pl...  7.79 us
    pallas_call x1, Pallas kernels, spread_call(): pl.pallas_call(functools.partial(spread_kernel, numbers=numbers), grid_sp...  5.54 us
  transfers between devices with their start and end apart: 4, of which 3 were waited for; matrix products, arithmetic and copies ran while one was open for 3% of the time, Pallas kernels for 2%

profile of v5, /device:TPU:1, one launch (start us, length us, event | category | flops | bytes accessed | tf_op | source)
XLA Modules:
  0.0 181.6 jit_solution(13707520121657634378)
XLA Ops:
  7.2 0.0 copy-start.1
  7.2 0.0 copy-start.7
  7.2 0.0 all-gather.2.cloned.1.call-start
  7.2 0.7 all-gather.2.cloned.1.call-update
  7.9 0.7 slice_bitcast_fusion.1
  8.6 0.2 copy.48.row_column_ref
  8.9 0.9 copy.47.tile_column_ref
  9.8 0.0 copy-start.2
  9.8 0.7 copy-done.2
  10.5 0.0 copy-start.4
  10.5 0.7 copy-done.4
  11.2 0.0 copy-start.5
  11.2 0.7 copy-done.5
  11.9 3.7 %shard_map.94 = (f32[64,4,128]{2,1,0:T(4,128)}, f32[1,1024]{1,0:T(1,128)S(1)}) custom-call(s32[1,1024]{1,0:T(1,128)S(1)} %bitcast.40, s32[2,1024]{1,0:T(2,128)S(1)} %copy-done.4, f32[2,1024]{1,0:T(2,128)S(1)} %copy-done.5, s32[1024,1]{1,0:T(8,128)S(1)} %copy.47.tile_column_ref, s32[1024,1]{1,0:T(8,128)S(1)} %copy.48.row_column_ref), custom_call_target="tpu_custom_call" | custom-call | tf_op jit(solution)/shard_map/pallas_call | solution.py:390
  15.6 14.8 %all-to-all-start = ((f32[64,4,128]{2,1,0:T(4,128)}), f32[64,4,128]{2,1,0:T(4,128)S(1)}, u32[]{:S(2)}, u32[]{:S(2)}) async-start(f32[64,4,128]{2,1,0:T(4,128)} %get-tuple-element.12), calls=%async_computation | async-start | bytes 262144 | tf_op jit(solution)/shard_map/all_to_all | solution.py:361
  30.4 0.0 copy-done.1
  30.4 0.1 copy.50
  30.6 0.0 copy-done.7
  30.6 10.2 %all-to-all-done = f32[64,4,128]{2,1,0:T(4,128)S(1)} async-done(((f32[64,4,128]{2,1,0:T(4,128)}), f32[64,4,128]{2,1,0:T(4,128)S(1)}, u32[]{:S(2)}, u32[]{:S(2)}) %all-to-all-start) | async-done | bytes 131104 | tf_op jit(solution)/shard_map/all_to_all | solution.py:361
  40.8 0.1 copy.57
  40.9 0.0 copy-start.3
  40.9 0.0 copy-start.6
  40.9 0.1 reshape.87.info_ref
  41.1 0.1 convert_element_type.40
  41.2 0.1 fusion.2
  41.3 0.1 reduce_min.26
  41.4 0.1 reduce_max.26
  41.4 0.1 gt.19
  41.5 0.1 reduce_min.27
  41.6 0.1 reduce_max.27
  41.8 0.3 select_reduce_fusion.1
  42.1 13.5 %all-gather.2.cloned.1.call-done.grid_ref = bf16[256,4096]{1,0:T(8,128)(2,1)} async-done(((bf16[32,4096]{1,0:T(8,128)(2,1)}), bf16[256,4096]{1,0:T(8,128)(2,1)}) %all-gather.2.cloned.1.call-update) | async-done | bytes 2097168 | tf_op jit(solution)/shard_map/all_gather | solution.py:388
  55.6 0.0 copy-start
  55.6 1.6 copy-done
  57.2 7.8 %shard_map.95 = (bf16[256,4096]{1,0:T(8,128)(2,1)S(1)}, f32[4,4096]{1,0:T(4,128)S(1)}) custom-call(s32[4,4]{1,0:T(4,128)S(1)} %pad_add_fusion.bounds_ref, f32[8,4096]{1,0:T(8,128)S(1)} %reshape.87.info_ref, bf16[256,4096]{1,0:T(8,128)(2,1)S(1)} %copy-done, bf16[512,256]{1,0:T(8,128)(2,1)S(1)} %bitcast.37, bf16[16,512]{1,0:T(8,128)(2,1)S(1)} %pad_bitcast_fusion.second_t_ref), custom_call_target="tpu_custom_call" | custom-call | tf_op jit(solution)/shard_map/pallas_call | solution.py:174
  65.0 0.1 reshape.88
  65.1 0.1 copy.58
  65.2 24.4 %all_to_all.30 = f32[64,2,128]{2,1,0:T(2,128)S(1)} all-to-all(f32[64,2,128]{2,1,0:T(2,128)S(1)} %copy.58), channel_id=1, replica_groups=mesh['tile'=64,'dp'=8] {'tile'}, dimensions={0} | all-to-all | bytes 131072 | tf_op jit(solution)/shard_map/all_to_all | solution.py:361
  89.6 0.0 copy-done.3
  89.6 0.0 copy-done.6
  89.6 2.6 %shard_map.96 = f32[64,2,128]{2,1,0:T(2,128)} custom-call(s32[1,1024]{1,0:T(1,128)S(1)} %bitcast.41, f32[1,1024]{1,0:T(1,128)S(1)} %get-tuple-element.13.slot_ref, f32[64,256]{1,0:T(8,128)S(1)} %bitcast.39, f32[3,64]{1,0:T(4,128)S(1)} %copy-done.6), custom_call_target="tpu_custom_call" | custom-call | tf_op jit(solution)/shard_map/pallas_call | solution.py:409
  92.2 4.4 %all-to-all-start.2 = ((f32[64,2,128]{2,1,0:T(2,128)}), f32[64,2,128]{2,1,0:T(2,128)S(1)}, u32[]{:S(2)}, u32[]{:S(2)}) async-start(f32[64,2,128]{2,1,0:T(2,128)} %shard_map.96), calls=%async_computation.2 | async-start | bytes 131072 | tf_op jit(solution)/shard_map/all_to_all | solution.py:361
  96.7 0.3 reduce-scatter.2.cloned.1.call-start
  96.9 0.1 copy.53.second_ref
  97.1 9.5 %all-to-all-done.2 = f32[64,2,128]{2,1,0:T(2,128)S(1)} async-done(((f32[64,2,128]{2,1,0:T(2,128)}), f32[64,2,128]{2,1,0:T(2,128)S(1)}, u32[]{:S(2)}, u32[]{:S(2)}) %all-to-all-start.2) | async-done | bytes 65568 | tf_op jit(solution)/shard_map/all_to_all | solution.py:361
  106.6 0.1 copy.59
  106.7 0.1 reshape.92.grads_ref
  106.8 8.2 %shard_map.97 = (bf16[256,4096]{1,0:T(8,128)(2,1)S(1)}, bf16[256,512]{1,0:T(8,128)(2,1)S(1)}, f32[4,512]{1,0:T(4,128)S(1)}) custom-call(f32[4,4096]{1,0:T(4,128)S(1)} %reshape.92.grads_ref, bf16[256,4096]{1,0:T(8,128)(2,1)S(1)} %get-tuple-element.15.features_ref, bf16[512,256]{1,0:T(8,128)(2,1)S(1)} %bitcast.38, bf16[256,512]{1,0:T(8,128)(2,1)S(1)} %copy-done.1, ...), custom_call_target="tpu_custom_call" | custom-call | tf_op jit(solution)/shard_map/pallas_call | solution.py:296
  115.0 5.5 %shard_map.98 = f32[256,4096]{1,0:T(8,128)} custom-call(s32[4,4]{1,0:T(4,128)S(1)} %pad_add_fusion.bounds_ref, f32[8,4096]{1,0:T(8,128)S(1)} %reshape.87.info_ref, bf16[256,4096]{1,0:T(8,128)(2,1)S(1)} %get-tuple-element.16.grads_ref), custom_call_target="tpu_custom_call" | custom-call | tf_op jit(solution)/shard_map/pallas_call | solution.py:346
  120.5 0.0 reduce-scatter.2.cloned.1.call-update
  120.5 0.1 reshape.93
  120.6 0.1 reshape.94
  120.7 0.1 copy.61
  120.8 0.2 fusion.1
  121.0 18.1 %all_to_all.31 = bf16[64,4,640]{2,1,0:T(4,128)(2,1)S(1)} all-to-all(bf16[64,4,640]{2,1,0:T(4,128)(2,1)S(1)} %fusion.1), channel_id=1, replica_groups=mesh['tile'=64,'dp'=8] {'tile'}, dimensions={0} | all-to-all | bytes 655360 | tf_op jit(solution)/shard_map/all_to_all | solution.py:361
  139.1 0.2 convert_reduce_fusion
  139.2 13.3 %all_to_all.32 = f32[8,4,640]{2,1,0:T(4,128)S(1)} all-to-all(f32[8,4,640]{2,1,0:T(4,128)S(1)} %broadcast_in_dim.39), channel_id=1, replica_groups=mesh['tile'=64,'dp'=8] {'dp'}, dimensions={0} | all-to-all | bytes 163840 | tf_op jit(solution)/shard_map/all_to_all | solution.py:373
  152.6 0.1 broadcast_in_dim.40
  152.7 20.2 %all_to_all.33 = bf16[64,4,640]{2,1,0:T(4,128)(2,1)S(1)} all-to-all(bf16[64,4,640]{2,1,0:T(4,128)(2,1)S(1)} %broadcast_in_dim.40), channel_id=1, replica_groups=mesh['tile'=64,'dp'=8] {'tile'}, dimensions={0} | all-to-all | bytes 655360 | tf_op jit(solution)/shard_map/all_to_all | solution.py:361
  172.9 1.0 reshape.95
  174.0 0.7 reshape.96
  174.7 0.0 reduce-scatter.2.cloned.1.call-done
  (16 shorter events, 0.2 us)
Async XLA Ops:
  7.2 23.3 %copy-start.1 = (bf16[256,512]{1,0:T(8,128)(2,1)S(1)}, bf16[256,512]{1,0:T(8,128)(2,1)}, u32[]{:S(2)}) copy-start(bf16[256,512]{1,0:T(8,128)(2,1)} %first_ref.1) | copy-start | bytes 786436
  7.2 23.4 %copy-start.7 = (bf16[512,4]{0,1:T(4,128)(2,1)S(1)}, bf16[512,4]{0,1:T(4,128)(2,1)}, u32[]{:S(2)}) copy-start(bf16[512,4]{0,1:T(4,128)(2,1)} %param.13) | copy-start | bytes 12292
  7.2 48.4 %all-gather.2.cloned.1.call-start = ((), (), s32[]{:S(2)}) async-start(), calls=%async_computation.7 | async-start | bytes 2359296 | tf_op jit(solution)/shard_map/all_gather | solution.py:388
  9.8 0.7 copy-start.2
  10.5 0.7 copy-start.4
  11.2 0.7 copy-start.5
  15.6 25.2 %all-to-all-start = ((f32[64,4,128]{2,1,0:T(4,128)}), f32[64,4,128]{2,1,0:T(4,128)S(1)}, u32[]{:S(2)}, u32[]{:S(2)}) async-start(f32[64,4,128]{2,1,0:T(4,128)} %get-tuple-element.12), calls=%async_computation | async-start | bytes 262144 | tf_op jit(solution)/shard_map/all_to_all | solution.py:361
  40.9 48.7 %copy-start.3 = (s32[1024,1]{0,1:T(1,128)S(1)}, s32[1024,1]{0,1:T(1,128)}, u32[]{:S(2)}) copy-start(s32[1024,1]{0,1:T(1,128)} %param.7) | copy-start | bytes 12292
  40.9 48.7 %copy-start.6 = (f32[3,64]{1,0:T(4,128)S(1)}, f32[3,64]{1,0:T(4,128)}, u32[]{:S(2)}) copy-start(f32[3,64]{1,0:T(4,128)} %targets_ref.1) | copy-start | bytes 2308
  55.6 1.6 copy-start
  92.2 14.3 %all-to-all-start.2 = ((f32[64,2,128]{2,1,0:T(2,128)}), f32[64,2,128]{2,1,0:T(2,128)S(1)}, u32[]{:S(2)}, u32[]{:S(2)}) async-start(f32[64,2,128]{2,1,0:T(2,128)} %shard_map.96), calls=%async_computation.2 | async-start | bytes 131072 | tf_op jit(solution)/shard_map/all_to_all | solution.py:361
  96.7 78.1 %reduce-scatter.2.cloned.1.call-start = ((), (), s32[]{:S(2)}) async-start(), calls=%async_computation.8 | async-start | bytes 4718592 | tf_op jit(solution)/shard_map/reduce_scatter | solution.py:422
Sparse Core Ops, SparseCore 0:
  10.1 45.4 all-gather.1
  120.6 52.8 reduce-scatter.1

commit v6 on v5

--- a/solution.py
+++ b/solution.py
@@ -99,10 +99,6 @@
         yield a, jnp.where(row == float(a), upper, jnp.where(row == float(a - 1), lower, zero))
 
 
-def logistic(x):
-    return 0.5 + 0.5 * jnp.tanh(0.5 * x)
-
-
 WINDOWS = (16, 24, 32, 40, GSIDE)
 ALIGN = 4
 
@@ -141,7 +137,7 @@
 
 
 def forward_kernel(
-    bounds_ref, info_ref, grid_ref, first_t_ref, second_t_ref,
+    bounds_ref, info_ref, grid_ref, half_first_t_ref, second_t_ref,
     features_ref, decoded_ref, weights_ref, *, rows,
 ):
     row, upper, lower = sample_columns(info_ref[...].astype(bf16))
@@ -160,8 +156,8 @@
 
     step = pl.program_id(0)
     in_window(bounds_ref[0, step], bounds_ref[1, step], gather)
-    pre_act = matmul(first_t_ref[...], features_ref[...])
-    hidden = (pre_act * logistic(pre_act)).astype(bf16)
+    half = matmul(half_first_t_ref[...], features_ref[...])
+    hidden = (half + half * jnp.tanh(half)).astype(bf16)
     decoded_ref[...] = matmul(second_t_ref[...], hidden)[0:4]
 
 
@@ -262,7 +258,7 @@
 
 
 def backward_kernel(
-    grads_ref, features_ref, first_t_ref, first_ref, second_ref,
+    grads_ref, features_ref, half_first_t_ref, first_ref, second_ref,
     feature_grad_ref, grad_first_ref, grad_second_ref, first_sum, second_sum,
 ):
     @pl.when(pl.program_id(0) == 0)
@@ -271,13 +267,13 @@
         second_sum[...] = jnp.zeros_like(second_sum)
 
     features = features_ref[...]
-    pre_act = matmul(first_t_ref[...], features)
-    gate = logistic(pre_act)
-    active = pre_act * gate
-    hidden = active.astype(bf16)
+    half = matmul(half_first_t_ref[...], features)
+    bend = jnp.tanh(half)
+    product = half * bend
+    hidden = (half + product).astype(bf16)
     pieces = exact_pieces(grads_ref[...])
     hidden_grad = matmul(second_ref[...], pieces)
-    pre_grad = (hidden_grad * (gate + active * (1.0 - gate))).astype(bf16)
+    pre_grad = (hidden_grad * (0.5 + 0.5 * bend) * (1.0 + half - product)).astype(bf16)
     feature_grad_ref[...] = matmul(first_ref[...], pre_grad).astype(bf16)
     first_sum[...] += matmul(features, pre_grad, ((1,), (1,)))
     second_sum[...] += matmul(pieces, hidden, ((1,), (1,)))
@@ -372,9 +368,9 @@
     copies = jnp.broadcast_to(mine, (groups,) + mine.shape)
     shared = lax.all_to_all(copies, "dp", split_axis=0, concat_axis=0, tiled=True)
     summed = jnp.sum(shared, axis=0).astype(bf16)
-    everything = over_tile(jnp.broadcast_to(summed, (owners,) + summed.shape)).astype(f32)
-    first = everything[:, :, :hid].reshape(channels, hid)
-    second = everything[:, :, hid : hid + hid // owners].transpose(0, 2, 1).reshape(hid, 4)
+    everything = over_tile(jnp.broadcast_to(summed, (owners,) + summed.shape))
+    first = everything[:, :, :hid].reshape(channels, hid).astype(f32)
+    second = everything[:, :, hid : hid + hid // owners].transpose(0, 2, 1).reshape(hid, 4).astype(f32)
     return first, second
 
 
@@ -395,7 +391,7 @@
         ],
         compiler_params=pltpu.CompilerParams(vmem_limit_bytes=SMALL_VMEM_BYTES),
     )(tile_row, corners, offsets, tile_ids, corners[0].reshape(samples, 1))
-    first_t = w_first.T
+    half_first_t = 0.5 * w_first.T
     second_8 = jnp.pad(w_second, ((0, 0), (0, 4)))
     second_t = jnp.pad(second_8, ((0, 0), (0, 8))).T
     info = over_tile(send_info).reshape(owners, 8, capacity).transpose(1, 2, 0)
@@ -403,7 +399,7 @@
     block = 1024
     bounds = window_bounds(info, block)
 
-    features, decoded = forward_call(bounds, info, grid_table, first_t, second_t, block)
+    features, decoded = forward_call(bounds, info, grid_table, half_first_t, second_t, block)
 
     back = over_tile(decoded.reshape(4, capacity, owners).transpose(2, 0, 1).reshape(owners, 2, -1))
     send_grads = pl.pallas_call(
@@ -416,7 +412,7 @@
 
     second_24 = jnp.concatenate([second_8] * 3, axis=1)
     feature_grad, grad_first, grad_second = backward_call(
-        grads, features, first_t, w_first, second_24
+        grads, features, half_first_t, w_first, second_24
     )
     share = spread_call(bounds, info, feature_grad, cells, block)
     grid_grad = lax.psum_scatter(share, "dp", scatter_dimension=0, tiled=True)

time: 182 us -> 182 us (level)
    all_to_all x3, blocking collectives: 62.7 us -> 65.3 us  [over_tile(): return lax.all_to_all(x, 'tile', split_axis=0, concat_axis=0, tiled=True)]
where the time goes in v6:
time: 182 us
  blocking collectives  77.8 us (43%)
  waiting for transfers between devices  33.8 us (19%)
  Pallas kernels  26.8 us (15%)
  starting transfers between devices  19.6 us (11%)
  between operations  14.3 us (8%)
  local copies, waits for them, and re-layouts  8.83 us (5%)
    all_to_all x3, blocking collectives, over_tile(): return lax.all_to_all(x, 'tile', split_axis=0, concat_axis=0, tiled=True)  65.3 us
    all_to_all x2, waiting for transfers between devices, over_tile(): return lax.all_to_all(x, 'tile', split_axis=0, concat_axis=0, tiled=True)  19.6 us
    all_to_all x2, starting transfers between devices, over_tile(): return lax.all_to_all(x, 'tile', split_axis=0, concat_axis=0, tiled=True)  19.3 us
    all_gather x1, waiting for transfers between devices, body(): grid_table = lax.all_gather(grid, 'dp', axis=0, tiled=True)  13.5 us
    all_to_all x1, blocking collectives, all_sum(): lax.all_to_all(copies, 'dp', split_axis=0, concat_axis=0, tiled=True)  12.5 us
    pallas_call x1, Pallas kernels, backward_call(): pl.pallas_call(backward_kernel, grid=(slots // block,), in_specs=[pl.Bloc...  7.87 us
    pallas_call x1, Pallas kernels, forward_call(): pl.pallas_call(functools.partial(forward_kernel, rows=rows), grid_spec=pl...  7.06 us
    pallas_call x1, Pallas kernels, spread_call(): pl.pallas_call(functools.partial(spread_kernel, numbers=numbers), grid_sp...  5.59 us
  transfers between devices with their start and end apart: 4, of which 3 were waited for; matrix products, arithmetic and copies ran while one was open for 3% of the time, Pallas kernels for 2%

profile of v6, /device:TPU:1, one launch (start us, length us, event | category | flops | bytes accessed | tf_op | source)
XLA Modules:
  0.0 182.3 jit_solution(14747781283968019622)
XLA Ops:
  7.2 0.0 copy-start.7
  7.2 0.0 copy-start.1
  7.2 0.0 all-gather.2.cloned.1.call-start
  7.2 0.7 all-gather.2.cloned.1.call-update
  7.9 0.7 slice_bitcast_fusion
  8.6 0.2 copy.48.row_column_ref
  8.9 0.9 copy.47.tile_column_ref
  9.8 0.0 copy-start.2
  9.8 0.7 copy-done.2
  10.5 0.0 copy-start.4
  10.5 0.7 copy-done.4
  11.2 0.0 copy-start.5
  11.2 0.7 copy-done.5
  11.9 3.7 %shard_map.94 = (f32[64,4,128]{2,1,0:T(4,128)}, f32[1,1024]{1,0:T(1,128)S(1)}) custom-call(s32[1,1024]{1,0:T(1,128)S(1)} %bitcast.39, s32[2,1024]{1,0:T(2,128)S(1)} %copy-done.4, f32[2,1024]{1,0:T(2,128)S(1)} %copy-done.5, s32[1024,1]{1,0:T(8,128)S(1)} %copy.47.tile_column_ref, s32[1024,1]{1,0:T(8,128)S(1)} %copy.48.row_column_ref), custom_call_target="tpu_custom_call" | custom-call | tf_op jit(solution)/shard_map/pallas_call | solution.py:386
  15.6 14.8 %all-to-all-start = ((f32[64,4,128]{2,1,0:T(4,128)}), f32[64,4,128]{2,1,0:T(4,128)S(1)}, u32[]{:S(2)}, u32[]{:S(2)}) async-start(f32[64,4,128]{2,1,0:T(4,128)} %get-tuple-element.12), calls=%async_computation | async-start | bytes 262144 | tf_op jit(solution)/shard_map/all_to_all | solution.py:357
  30.4 0.0 copy-done.7
  30.5 0.0 copy-done.1
  30.5 0.1 copy.50
  30.6 10.1 %all-to-all-done = f32[64,4,128]{2,1,0:T(4,128)S(1)} async-done(((f32[64,4,128]{2,1,0:T(4,128)}), f32[64,4,128]{2,1,0:T(4,128)S(1)}, u32[]{:S(2)}, u32[]{:S(2)}) %all-to-all-start) | async-done | bytes 131104 | tf_op jit(solution)/shard_map/all_to_all | solution.py:357
  40.8 0.1 copy.57
  40.9 0.0 copy-start.3
  40.9 0.0 copy-start.6
  40.9 0.1 reshape.87.info_ref
  41.1 0.1 convert_element_type.52
  41.2 0.1 fusion.2
  41.3 0.1 reduce_min.26
  41.4 0.1 reduce_max.26
  41.4 0.1 gt.19
  41.5 0.1 reduce_min.27
  41.6 0.1 reduce_max.27
  41.8 0.3 select_reduce_fusion.1
  42.1 13.5 %all-gather.2.cloned.1.call-done.grid_ref = bf16[256,4096]{1,0:T(8,128)(2,1)} async-done(((bf16[32,4096]{1,0:T(8,128)(2,1)}), bf16[256,4096]{1,0:T(8,128)(2,1)}) %all-gather.2.cloned.1.call-update) | async-done | bytes 2097168 | tf_op jit(solution)/shard_map/all_gather | solution.py:384
  55.6 0.0 copy-start
  55.6 1.6 copy-done
  57.2 7.1 %shard_map.95 = (bf16[256,4096]{1,0:T(8,128)(2,1)S(1)}, f32[4,4096]{1,0:T(4,128)S(1)}) custom-call(s32[4,4]{1,0:T(4,128)S(1)} %pad_add_fusion.bounds_ref, f32[8,4096]{1,0:T(8,128)S(1)} %reshape.87.info_ref, bf16[256,4096]{1,0:T(8,128)(2,1)S(1)} %copy-done, bf16[512,256]{1,0:T(8,128)(2,1)S(1)} %multiply_bitcast_fusion.half_first_t_ref, ...), custom_call_target="tpu_custom_call" | custom-call | tf_op jit(solution)/shard_map/pallas_call | solution.py:170
  64.2 0.1 reshape.88
  64.4 0.1 copy.58
  64.5 26.4 %all_to_all.30 = f32[64,2,128]{2,1,0:T(2,128)S(1)} all-to-all(f32[64,2,128]{2,1,0:T(2,128)S(1)} %copy.58), channel_id=1, replica_groups=mesh['tile'=64,'dp'=8] {'tile'}, dimensions={0} | all-to-all | bytes 131072 | tf_op jit(solution)/shard_map/all_to_all | solution.py:357
  90.8 0.0 copy-done.3
  90.8 0.0 copy-done.6
  90.8 2.6 %shard_map.96 = f32[64,2,128]{2,1,0:T(2,128)} custom-call(s32[1,1024]{1,0:T(1,128)S(1)} %bitcast.40, f32[1,1024]{1,0:T(1,128)S(1)} %get-tuple-element.13.slot_ref, f32[64,256]{1,0:T(8,128)S(1)} %bitcast.38, f32[3,64]{1,0:T(4,128)S(1)} %copy-done.6), custom_call_target="tpu_custom_call" | custom-call | tf_op jit(solution)/shard_map/pallas_call | solution.py:405
  93.4 4.4 %all-to-all-start.2 = ((f32[64,2,128]{2,1,0:T(2,128)}), f32[64,2,128]{2,1,0:T(2,128)S(1)}, u32[]{:S(2)}, u32[]{:S(2)}) async-start(f32[64,2,128]{2,1,0:T(2,128)} %shard_map.96), calls=%async_computation.2 | async-start | bytes 131072 | tf_op jit(solution)/shard_map/all_to_all | solution.py:357
  97.9 0.3 reduce-scatter.2.cloned.1.call-start
  98.2 0.1 copy.53.second_ref
  98.3 9.5 %all-to-all-done.2 = f32[64,2,128]{2,1,0:T(2,128)S(1)} async-done(((f32[64,2,128]{2,1,0:T(2,128)}), f32[64,2,128]{2,1,0:T(2,128)S(1)}, u32[]{:S(2)}, u32[]{:S(2)}) %all-to-all-start.2) | async-done | bytes 65568 | tf_op jit(solution)/shard_map/all_to_all | solution.py:357
  107.8 0.1 copy.59
  107.9 0.1 reshape.92.grads_ref
  108.0 7.9 %shard_map.97 = (bf16[256,4096]{1,0:T(8,128)(2,1)S(1)}, bf16[256,512]{1,0:T(8,128)(2,1)S(1)}, f32[4,512]{1,0:T(4,128)S(1)}) custom-call(f32[4,4096]{1,0:T(4,128)S(1)} %reshape.92.grads_ref, bf16[256,4096]{1,0:T(8,128)(2,1)S(1)} %get-tuple-element.15.features_ref, bf16[512,256]{1,0:T(8,128)(2,1)S(1)} %multiply_bitcast_fusion.half_first_t_ref, ...), custom_call_target="tpu_custom_call" | custom-call | tf_op jit(solution)/shard_map/pallas_call | solution.py:292
  115.9 5.6 %shard_map.98 = f32[256,4096]{1,0:T(8,128)} custom-call(s32[4,4]{1,0:T(4,128)S(1)} %pad_add_fusion.bounds_ref, f32[8,4096]{1,0:T(8,128)S(1)} %reshape.87.info_ref, bf16[256,4096]{1,0:T(8,128)(2,1)S(1)} %get-tuple-element.16.grads_ref), custom_call_target="tpu_custom_call" | custom-call | tf_op jit(solution)/shard_map/pallas_call | solution.py:342
  121.5 0.0 reduce-scatter.2.cloned.1.call-update
  121.5 0.1 reshape.93
  121.6 0.1 reshape.94
  121.7 0.1 copy.61
  121.7 0.2 fusion.1
  121.9 18.6 %all_to_all.31 = bf16[64,4,640]{2,1,0:T(4,128)(2,1)S(1)} all-to-all(bf16[64,4,640]{2,1,0:T(4,128)(2,1)S(1)} %fusion.1), channel_id=1, replica_groups=mesh['tile'=64,'dp'=8] {'tile'}, dimensions={0} | all-to-all | bytes 655360 | tf_op jit(solution)/shard_map/all_to_all | solution.py:357
  140.5 0.2 convert_reduce_fusion
  140.7 12.5 %all_to_all.32 = f32[8,4,640]{2,1,0:T(4,128)S(1)} all-to-all(f32[8,4,640]{2,1,0:T(4,128)S(1)} %broadcast_in_dim.39), channel_id=1, replica_groups=mesh['tile'=64,'dp'=8] {'dp'}, dimensions={0} | all-to-all | bytes 163840 | tf_op jit(solution)/shard_map/all_to_all | solution.py:369
  153.3 0.1 broadcast_in_dim.40
  153.4 20.3 %all_to_all.33 = bf16[64,4,640]{2,1,0:T(4,128)(2,1)S(1)} all-to-all(bf16[64,4,640]{2,1,0:T(4,128)(2,1)S(1)} %broadcast_in_dim.40), channel_id=1, replica_groups=mesh['tile'=64,'dp'=8] {'tile'}, dimensions={0} | all-to-all | bytes 655360 | tf_op jit(solution)/shard_map/all_to_all | solution.py:357
  173.7 0.7 reshape.96
  174.5 1.0 reshape.95
  175.4 0.0 reduce-scatter.2.cloned.1.call-done
  (16 shorter events, 0.2 us)
Async XLA Ops:
  7.2 23.3 %copy-start.7 = (bf16[512,4]{0,1:T(4,128)(2,1)S(1)}, bf16[512,4]{0,1:T(4,128)(2,1)}, u32[]{:S(2)}) copy-start(bf16[512,4]{0,1:T(4,128)(2,1)} %param.13) | copy-start | bytes 12292
  7.2 23.3 %copy-start.1 = (bf16[256,512]{1,0:T(8,128)(2,1)S(1)}, bf16[256,512]{1,0:T(8,128)(2,1)}, u32[]{:S(2)}) copy-start(bf16[256,512]{1,0:T(8,128)(2,1)} %first_ref.1) | copy-start | bytes 786436
  7.2 48.4 %all-gather.2.cloned.1.call-start = ((), (), s32[]{:S(2)}) async-start(), calls=%async_computation.7 | async-start | bytes 2359296 | tf_op jit(solution)/shard_map/all_gather | solution.py:384
  9.8 0.7 copy-start.2
  10.5 0.7 copy-start.4
  11.2 0.7 copy-start.5
  15.6 25.2 %all-to-all-start = ((f32[64,4,128]{2,1,0:T(4,128)}), f32[64,4,128]{2,1,0:T(4,128)S(1)}, u32[]{:S(2)}, u32[]{:S(2)}) async-start(f32[64,4,128]{2,1,0:T(4,128)} %get-tuple-element.12), calls=%async_computation | async-start | bytes 262144 | tf_op jit(solution)/shard_map/all_to_all | solution.py:357
  40.9 49.9 %copy-start.3 = (s32[1024,1]{0,1:T(1,128)S(1)}, s32[1024,1]{0,1:T(1,128)}, u32[]{:S(2)}) copy-start(s32[1024,1]{0,1:T(1,128)} %param.7) | copy-start | bytes 12292
  40.9 49.9 %copy-start.6 = (f32[3,64]{1,0:T(4,128)S(1)}, f32[3,64]{1,0:T(4,128)}, u32[]{:S(2)}) copy-start(f32[3,64]{1,0:T(4,128)} %targets_ref.1) | copy-start | bytes 2308
  55.6 1.6 copy-start
  93.4 14.3 %all-to-all-start.2 = ((f32[64,2,128]{2,1,0:T(2,128)}), f32[64,2,128]{2,1,0:T(2,128)S(1)}, u32[]{:S(2)}, u32[]{:S(2)}) async-start(f32[64,2,128]{2,1,0:T(2,128)} %shard_map.96), calls=%async_computation.2 | async-start | bytes 131072 | tf_op jit(solution)/shard_map/all_to_all | solution.py:357
  97.9 77.6 %reduce-scatter.2.cloned.1.call-start = ((), (), s32[]{:S(2)}) async-start(), calls=%async_computation.8 | async-start | bytes 4718592 | tf_op jit(solution)/shard_map/reduce_scatter | solution.py:418
Sparse Core Ops, SparseCore 0:
  10.1 45.4 all-gather.1
  121.6 52.6 reduce-scatter.1
